TPU v7x, 256 devices: a whole 4x4x8 slice. The times are simulated.
256 devices in a mesh: node: 16 (over z_lo, x, core), dp: 16 (over z_hi, y).
Axes of the slice: x: 4, y: 4, z: 8 (z_hi: 4, z_lo: 2; z = z_hi * 2 + z_lo), core: 2. Of those that a mesh axis runs over, the one named last changes fastest.
Arguments:
- tokens: bfloat16 [65536, 8192], P(('node', 'dp')), may hold values from -24 to 24
- norm_gain: float32 [8192], replicated, may hold values from 0.5 to 1.5
- value_weight: bfloat16 [8192, 512], P('dp'), may hold values from -0.0625 to 0.0625
- value_grads: bfloat16 [65536, 512], P(('node', 'dp')), may hold values from -48 to 48
- new_logprobs: float32 [65536], P(('node', 'dp')), may hold values from -1.2 to 1.2
- old_logprobs: float32 [65536], P(('node', 'dp')), may hold values from -1.2 to 1.2
- advantages: float32 [512], P(('node', 'dp')), may hold values from -4 to 4
- lengths: int32 [512], P(('node', 'dp')), may hold values from 1 to 128
Outputs:
- input_grads: bfloat16 [65536, 8192], P(('node', 'dp'))
- weight_grads: float32 [8192, 512], P('dp')
- gain_grads: float32 [8192], replicated
All inputs are finite; a program needn't handle non-finite values.
Results may differ from a plain program's by a relative error of at most 0.0051.
Values may be sent and summed in bfloat16 or wider, within the bound.
A program may use at most 128 MiB of HBM per device.

v0:
```python
import jax
import jax.numpy as jnp
from jax import lax
from jax.sharding import PartitionSpec as P

SEQ = 128
BLOCK = 64


epsilon = 1e-06


def block_terms(tokens_block, cotan_block, norm_gain, full_weight):
    wide_tokens = tokens_block.astype(jnp.float32)
    inverse_rms = lax.rsqrt(jnp.mean(wide_tokens * wide_tokens, axis=-1, keepdims=True) + epsilon)
    normed = (wide_tokens * inverse_rms * norm_gain).astype(jnp.bfloat16)
    normed_grad = lax.dot_general(
        cotan_block, full_weight, (((1,), (1,)), ((), ())), preferred_element_type=jnp.float32
    )
    scaled_grad = norm_gain * normed_grad
    cubed = inverse_rms * inverse_rms * inverse_rms
    input_grad = inverse_rms * scaled_grad - wide_tokens * cubed * jnp.mean(
        wide_tokens * scaled_grad, axis=-1, keepdims=True
    )
    gain_part = jnp.sum(normed_grad * wide_tokens * inverse_rms, axis=0)
    return (normed, input_grad.astype(jnp.bfloat16), gain_part)


def on_device(
    tokens, norm_gain, value_weight, value_grads, new_logprobs, old_logprobs, advantages, lengths
):
    row_count, feature_count = tokens.shape
    value_count = value_grads.shape[1]
    seq_count = lengths.shape[0]
    length_rows = jnp.broadcast_to(lengths[:, None], (seq_count, SEQ)).reshape(row_count)
    advantage_rows = jnp.broadcast_to(advantages[:, None], (seq_count, SEQ)).reshape(row_count)
    positions = jnp.arange(row_count, dtype=jnp.int32) % SEQ
    alive = (positions < length_rows).astype(jnp.int32)
    ratios = jnp.exp(new_logprobs - old_logprobs)
    token_weight = -advantage_rows * jnp.clip(ratios, 0.8, 1.2) / SEQ * alive.astype(jnp.float32)
    value_cotan = (token_weight[:, None] * value_grads.astype(jnp.float32)).astype(jnp.bfloat16)
    full_weight = lax.all_gather(value_weight, "dp", axis=0, tiled=True)
    block_count = row_count // BLOCK
    block_alive = jnp.sum(alive.reshape(block_count, BLOCK), axis=1) > 0

    def compute_block(tokens_block, cotan_block):
        return block_terms(tokens_block, cotan_block, norm_gain, full_weight)

    def empty_block(tokens_block, cotan_block):
        return (
            jnp.zeros(tokens_block.shape, jnp.bfloat16),
            jnp.zeros(tokens_block.shape, jnp.bfloat16),
            jnp.zeros((tokens_block.shape[1],), jnp.float32),
        )

    def each_block(item):
        tokens_block, cotan_block, flagged = item
        return lax.cond(flagged, compute_block, empty_block, tokens_block, cotan_block)

    normed, grads_inner, gain_parts = lax.map(
        each_block,
        (
            tokens.reshape(block_count, BLOCK, feature_count),
            value_cotan.reshape(block_count, BLOCK, value_count),
            block_alive,
        ),
    )
    normed = normed.reshape(row_count, feature_count)
    input_grads = grads_inner.reshape(row_count, feature_count)
    gain_local = jnp.sum(gain_parts, axis=0)
    local_sum = lax.psum_scatter(
        jnp.einsum("rd,rv->dv", normed, value_cotan, preferred_element_type=jnp.float32),
        "dp",
        scatter_dimension=0,
        tiled=True,
    )
    weight_total = lax.psum(local_sum, "node")
    gain_total = lax.psum(gain_local, ("node", "dp"))
    return (input_grads, weight_total, gain_total)


def solution(mesh):
    in_specs = (
        P(("node", "dp"), None),
        P(),
        P("dp", None),
        P(("node", "dp"), None),
        P(("node", "dp")),
        P(("node", "dp")),
        P(("node", "dp")),
        P(("node", "dp")),
    )
    out_specs = (P(("node", "dp"), None), P("dp", None), P())
    return jax.shard_map(
        on_device, mesh=mesh, in_specs=in_specs, out_specs=out_specs, check_vma=False
    )
```

profile of v0, /device:TPU:1, one launch (start us, length us, event | category | flops | bytes accessed | tf_op | source)
XLA Modules:
  0.0 529.9 jit_solution(10693161780965337216)
XLA Ops:
  7.2 0.0 all-gather.2.cloned.1.call-start
  7.2 0.7 all-gather.2.cloned.1.call-update
  7.9 0.0 reduce-scatter.2.cloned.1.call-start
  8.0 0.7 neg.7
  8.6 0.7 broadcast_in_dim.51
  9.4 0.1 broadcast_in_dim.52
  9.4 0.2 convert_reduce_fusion
  9.6 0.8 fusion.21
  10.4 1.1 multiply_convert_fusion
  11.5 113.8 %all-gather.2.cloned.1.call-done = bf16[8192,512]{1,0:T(8,128)(2,1)} async-done(((bf16[512,512]{1,0:T(8,128)(2,1)}), bf16[8192,512]{1,0:T(8,128)(2,1)}) %all-gather.2.cloned.1.call-update) | async-done | bytes 8388624 | tf_op jit(solution)/shard_map/all_gather | solution.py:42
  125.2 31.2 %while.14 = (s32[]{:T(128)}, bf16[4,64,8192]{2,1,0:T(8,128)(2,1)}, bf16[4,64,8192]{2,1,0:T(8,128)(2,1)}, f32[4,8192]{1,0:T(4,128)S(1)}, pred[4]{0:T(512)(128)(4,...) while((s32[]{:T(128)}, bf16[4,64,8192]{2,1,0:T(8,128)(2,1)}, ...), condition=%wide.region_7.8_spmd, body=%wide.region_1.7_spmd.sunk | while | flops 547872960 | bytes 40244232 | solution.py:60
  125.2 0.6 dynamic_slice.34
  126.4 9.1 %conditional.2 = (bf16[1,64,8192]{2,1,0:T(8,128)(2,1)S(1)}, bf16[1,64,8192]{2,1,0:T(8,128)(2,1)S(1)}, f32[1,8192]{1,0:T(1,128)S(1)}) conditional(s32[]{:T(128)} %bitcast.55, () %tuple.48, (bf16[4,64,8192]{2,1,0:T(8,128)(2,1)}, s32[]{:T(128)}, f32[8192]{0:T(1024)}, bf16[4,64,512]{2,1,0:T(8,128)(2,1)S(1)}, bf16[8192,512]{1,0:T(8,128)(2,1)}) %tuple.49), branch_computations={%region_2.2_spmd, %region_3.6_spmd} | conditional | flops 547872960 | bytes 35983708 | solution.py:58
  126.4 1.5 fusion.4
  128.0 6.7 %fusion.10 = (f32[8192]{0:T(1024)S(1)}, f32[64]{0:T(128)S(1)}, f32[64,8192]{1,0:T(8,128)S(1)}) fusion(f32[64]{0:T(128)S(1)} %get-tuple-element.128, bf16[4,64,8192]{2,1,0:T(8,128)(2,1)} %get-tuple-element.80, s32[]{:T(128)} %get-tuple-element.81, f32[8192]{0:T(1024)} %get-tuple-element.82, bf16[8192,512]{1,0:T(8,128)(2,1)} %get-tuple-element.84, ...), kind=kOutput, calls=%fused_computation.12 | convolution fusion | flops 540532672 | bytes 11667200 | tf_op jit(solution)/shard_map/while/body/eval_jaxpr/cond/branch_1_fun/dot_general | solution.py:17
  134.7 0.5 fusion.13
  135.2 0.3 fusion.12
  135.5 0.5 dynamic_update_slice.16
  136.0 1.5 constant_dynamic-update-slice_fusion.3
  137.5 0.6 dynamic_slice.34
  138.6 0.2 conditional.2
  138.6 0.1 broadcast_in_dim.40.clone
  138.7 0.1 broadcast_in_dim.40
  138.8 0.5 dynamic_update_slice.16
  139.3 1.5 constant_dynamic-update-slice_fusion.3
  140.8 0.6 dynamic_slice.34
  142.0 9.1 %conditional.2 = (bf16[1,64,8192]{2,1,0:T(8,128)(2,1)S(1)}, bf16[1,64,8192]{2,1,0:T(8,128)(2,1)S(1)}, f32[1,8192]{1,0:T(1,128)S(1)}) conditional(s32[]{:T(128)} %bitcast.55, () %tuple.48, (bf16[4,64,8192]{2,1,0:T(8,128)(2,1)}, s32[]{:T(128)}, f32[8192]{0:T(1024)}, bf16[4,64,512]{2,1,0:T(8,128)(2,1)S(1)}, bf16[8192,512]{1,0:T(8,128)(2,1)}) %tuple.49), branch_computations={%region_2.2_spmd, %region_3.6_spmd} | conditional | flops 547872960 | bytes 35983708 | solution.py:58
  142.0 1.5 fusion.4
  143.6 6.7 %fusion.10 = (f32[8192]{0:T(1024)S(1)}, f32[64]{0:T(128)S(1)}, f32[64,8192]{1,0:T(8,128)S(1)}) fusion(f32[64]{0:T(128)S(1)} %get-tuple-element.128, bf16[4,64,8192]{2,1,0:T(8,128)(2,1)} %get-tuple-element.80, s32[]{:T(128)} %get-tuple-element.81, f32[8192]{0:T(1024)} %get-tuple-element.82, bf16[8192,512]{1,0:T(8,128)(2,1)} %get-tuple-element.84, ...), kind=kOutput, calls=%fused_computation.12 | convolution fusion | flops 540532672 | bytes 11667200 | tf_op jit(solution)/shard_map/while/body/eval_jaxpr/cond/branch_1_fun/dot_general | solution.py:17
  150.3 0.5 fusion.13
  150.8 0.3 fusion.12
  151.1 0.5 dynamic_update_slice.16
  151.6 1.5 constant_dynamic-update-slice_fusion.3
  153.1 0.6 dynamic_slice.34
  154.2 0.2 conditional.2
  154.2 0.1 broadcast_in_dim.40.clone
  154.3 0.1 broadcast_in_dim.40
  154.4 0.5 dynamic_update_slice.16
  154.9 1.5 constant_dynamic-update-slice_fusion.3
  156.4 10.3 %fusion.23 = f32[8192,512]{1,0:T(8,128)} fusion(bf16[256,8192]{1,0:T(8,128)(2,1)} %bitcast.57, bf16[256,512]{1,0:T(8,128)(2,1)S(1)} %bitcast.60), kind=kOutput, calls=%fused_computation.39 | convolution fusion | flops 2147483648 | bytes 21233664 | tf_op jit(solution)/shard_map/rd,rv->dv/dot_general | solution.py:72
  166.7 0.0 reduce-scatter.2.cloned.1.call-update
  166.7 0.0 all-reduce.2.cloned.1.call-start
  166.7 229.3 %reduce-scatter.2.cloned.1.call-done = f32[512,512]{1,0:T(8,128)} async-done(((f32[8192,512]{1,0:T(8,128)}), f32[512,512]{1,0:T(8,128)}) %reduce-scatter.2.cloned.1.call-update) | async-done | bytes 1048592 | tf_op jit(solution)/shard_map/reduce_scatter | solution.py:71
  396.1 0.0 all-reduce.2.cloned.1.call-update
  396.1 0.1 reduce_sum.52
  396.2 75.7 %psum.15 = f32[8192]{0:T(1024)} all-reduce(f32[8192]{0:T(1024)S(1)} %reduce_sum.52), channel_id=1, replica_groups=mesh['node'=16,'dp'=16] {'node','dp'}, use_global_device_ids=true, to_apply=%region_11.12 | all-reduce | flops 8192 | bytes 65536 | tf_op jit(solution)/shard_map/psum | solution.py:78
  471.9 49.2 %all-reduce.2.cloned.1.call-done = f32[512,512]{1,0:T(8,128)} async-done(((f32[512,512]{1,0:T(8,128)}), f32[512,512]{1,0:T(8,128)}) %all-reduce.2.cloned.1.call-update) | async-done | bytes 1048592 | tf_op jit(solution)/shard_map/psum | solution.py:77
  521.1 2.3 copy.33
  (18 shorter events, 0.1 us)
Async XLA Ops:
  7.2 118.1 %all-gather.2.cloned.1.call-start = ((), (), s32[]{:S(2)}) async-start(), calls=%async_computation.1 | async-start | bytes 8912896 | tf_op jit(solution)/shard_map/all_gather | solution.py:42
  7.9 388.2 %reduce-scatter.2.cloned.1.call-start = ((), (), s32[]{:S(2)}) async-start(), calls=%async_computation.2 | async-start | bytes 17825792 | tf_op jit(solution)/shard_map/reduce_scatter | solution.py:71
  127.9 6.7 %copy-start = (bf16[4,64,8192]{2,1,0:T(8,128)(2,1)S(1)}, bf16[4,64,8192]{2,1,0:T(8,128)(2,1)}, u32[]{:S(2)}) copy-start(bf16[4,64,8192]{2,1,0:T(8,128)(2,1)} %get-tuple-element.80) | copy-start | bytes 12582916 | tf_op jit(solution)/shard_map/while/body/eval_jaxpr/cond
  127.9 6.7 %copy-start.1 = (f32[8192]{0:T(1024)S(1)}, f32[8192]{0:T(1024)}, u32[]{:S(2)}) copy-start(f32[8192]{0:T(1024)} %get-tuple-element.82) | copy-start | bytes 98308 | tf_op jit(solution)/shard_map/while/body/eval_jaxpr/cond
  143.5 6.7 %copy-start = (bf16[4,64,8192]{2,1,0:T(8,128)(2,1)S(1)}, bf16[4,64,8192]{2,1,0:T(8,128)(2,1)}, u32[]{:S(2)}) copy-start(bf16[4,64,8192]{2,1,0:T(8,128)(2,1)} %get-tuple-element.80) | copy-start | bytes 12582916 | tf_op jit(solution)/shard_map/while/body/eval_jaxpr/cond
  143.6 6.7 %copy-start.1 = (f32[8192]{0:T(1024)S(1)}, f32[8192]{0:T(1024)}, u32[]{:S(2)}) copy-start(f32[8192]{0:T(1024)} %get-tuple-element.82) | copy-start | bytes 98308 | tf_op jit(solution)/shard_map/while/body/eval_jaxpr/cond
  166.7 354.4 %all-reduce.2.cloned.1.call-start = ((), (), s32[]{:S(2)}) async-start(), calls=%async_computation.3 | async-start | bytes 2097152 | tf_op jit(solution)/shard_map/psum | solution.py:77
Sparse Core Ops, SparseCore 0:
  10.4 114.7 all-gather.1
  166.8 229.2 reduce-scatter.1
  398.7 122.3 all-reduce.1
where the time goes:
time: 530 us
  waiting for transfers between devices  393 us (74%)
  blocking collectives  75.7 us (14%)
  matrix products  23.6 us (4%)
  between operations  13.8 us (3%)
  local copies, waits for them, and re-layouts  13.6 us (3%)
  other arithmetic  7.48 us (1%)
    reduce_scatter x1, waiting for transfers between devices, on_device(): lax.psum_scatter(jnp.einsum('rd,rv->dv', normed, value_cotan, preferred_e...  229 us
    all_gather x1, waiting for transfers between devices, on_device(): full_weight = lax.all_gather(value_weight, 'dp', axis=0, tiled=True)  114 us
    psum x1, blocking collectives, on_device(): gain_total = lax.psum(gain_local, ('node', 'dp'))  75.7 us
    psum x1, waiting for transfers between devices, on_device(): weight_total = lax.psum(local_sum, 'node')  49.2 us
    dot_general x2, matrix products, block_terms(): lax.dot_general(cotan_block, full_weight, (((1,), (1,)), ((), ())), prefe...  13.4 us
  transfers between devices with their start and end apart: 3, of which 3 were waited for; matrix products, arithmetic and copies ran while one was open for 1% of the time, Pallas kernels for 0%

commit v1 on v0

v1 whole, which is shorter than its diff:
```python
import functools

import jax
import jax.numpy as jnp
from jax import lax
from jax.experimental import pallas as pl
from jax.experimental.pallas import tpu as pltpu
from jax.sharding import PartitionSpec as P

SEQ = 128
EPS = 1e-06
K = 8
R = 128 // K
CUT = 192
MESH = pl.DeviceIdType.MESH
F32 = jnp.float32
BF16 = jnp.bfloat16


def mod(a, n):
    return lax.rem(a + 2 * n, n)


def kernel(
    tok_hbm, gain_ref, w_hbm, vg_ref, new_ref, old_ref, adv_ref, len_ref,
    ig_hbm, wg_ref, gg_ref,
    tok, wfull, ngs, nown, nsend, nrecv, cot, cot_t, cot_t_in, inv_ref, acc,
    part, xin_a, xin_b, xin_c, yin, ts, zin, wt,
    gpart, gcore, gx, gy, gz,
    lsem, ssem, rsem,
):
    node = lax.axis_index("node")
    dp = lax.axis_index("dp")
    c = lax.rem(node, 2)
    x = lax.rem(node // 2, 4)
    lo = node // 8
    h = dp // 4
    y = lax.rem(dp, 4)
    z = 2 * h + lo
    j_me = dp

    def dev(x=x, y=y, z=z, c=c):
        return (lax.rem(z, 2) * 8 + x * 2 + c, (z // 2) * 4 + y)

    sgn = 2 * lo - 1
    z_out = mod(z + sgn, 8)
    z_mate = mod(z - sgn, 8)
    d_core = dev(c=1 - c)
    d_x = {1: dev(x=mod(x + 1, 4)), -1: dev(x=mod(x - 1, 4)), 2: dev(x=mod(x + 2, 4))}
    d_y = {1: dev(y=mod(y + 1, 4)), -1: dev(y=mod(y - 1, 4)), 2: dev(y=mod(y + 2, 4))}
    d_out = dev(z=z_out)
    d_mate = dev(z=z_mate)
    d_z = {d: dev(z=mod(z + d, 8)) for d in range(1, 8)}

    barrier = pltpu.get_barrier_semaphore()
    peers = [d_core, *d_x.values(), *d_y.values(), *d_z.values()]
    for peer in peers:
        pl.semaphore_signal(barrier, inc=1, device_id=peer, device_id_type=MESH)

    loads = []
    for r in range(4):
        loads.append(pltpu.make_async_copy(
            tok_hbm.at[pl.ds(r * 64, 64)], tok.at[pl.ds(r * 64, 64)], lsem.at[r]))
    wload = pltpu.make_async_copy(w_hbm, wfull.at[j_me], lsem.at[4])
    for cp in loads:
        cp.start()
    wload.start()

    names = {}
    sent = []

    def message(name, src, dst, device):
        index = names.setdefault(name, len(names))
        return pltpu.make_async_remote_copy(
            src_ref=src, dst_ref=dst, send_sem=ssem.at[index], recv_sem=rsem.at[index],
            device_id=device, device_id_type=MESH)

    waits = {}

    def send(name, src, dst, device):
        copy = message(name, src, dst, device)
        copy.start()
        sent.append(copy)
        waits[name] = copy

    def got(name):
        waits.pop(name).wait_recv()

    row = lax.broadcasted_iota(jnp.int32, (2, SEQ), 0)
    pos = lax.broadcasted_iota(jnp.int32, (2, SEQ), 1)
    adv = jnp.where(row == 0, adv_ref[0], adv_ref[1])
    length = jnp.where(row == 0, len_ref[0], len_ref[1])
    alive = (pos < length).astype(F32)
    ratio = jnp.exp(new_ref[...] - old_ref[...])
    weight = -adv * jnp.clip(ratio, 0.8, 1.2) / SEQ * alive
    eye = lax.broadcasted_iota(jnp.int32, (SEQ, SEQ), 0) == lax.broadcasted_iota(
        jnp.int32, (SEQ, SEQ), 1)
    for s in range(2):
        column = jnp.sum(jnp.where(eye, weight[s : s + 1, :], 0.0), axis=1, keepdims=True)
        wide = column * vg_ref[pl.ds(s * SEQ, SEQ), :].astype(F32)
        cot[pl.ds(s * SEQ, SEQ), :] = wide.astype(BF16)
        cot_t[:, pl.ds(s * SEQ, SEQ)] = wide.T.astype(BF16)

    for r in range(4):
        loads[r].wait()
        rows = pl.ds(r * 64, 64)

        def squares(i, total):
            part_ = tok[rows, pl.ds(pl.multiple_of(i * 512, 512), 512)].astype(F32)
            part_ = part_ * part_
            return total + ((part_[:, :128] + part_[:, 128:256])
                            + (part_[:, 256:384] + part_[:, 384:]))

        total = lax.fori_loop(0, 16, squares, jnp.zeros((64, 128), F32), unroll=2)
        mean = jnp.sum(total, axis=1, keepdims=True) / 8192.0
        inv_ref[rows, :] = jnp.broadcast_to(lax.rsqrt(mean + EPS), (64, 128))

    def inverse():
        return inv_ref[:, 0:1]

    def norm_block(block, dst, jj):
        lanes = pl.ds(pl.multiple_of(block * 256, 256), 256)
        value = tok[:, lanes].astype(F32) * inverse() * gain_ref[pl.ds(block, 1), :]
        dst[jj] = value.astype(BF16)

    @pl.loop(0, 16)
    def _(jj):
        norm_block(2 * jj + (1 - c), nsend, jj)

    wload.wait()
    pl.semaphore_wait(barrier, len(peers))

    events = []

    def at(time, fn):
        events.append((time, len(events), fn))

    send("cot", cot_t, cot_t_in, d_core)
    for g in range(4):
        send(("n", g), nsend.at[pl.ds(4 * g, 4)], nrecv.at[pl.ds(4 * g, 4)], d_core)

    deltas = (1, -1, 2)

    def wblock(hh, yy, lo_row, count):
        return wfull.at[mod(hh, 4) * 4 + mod(yy, 4), c, pl.ds(lo_row, count)]

    core_waits = []

    def to_core(name, ref):
        send(("k", name), ref, ref, d_core)
        core_waits.append(("k", name))

    def half_rows(unit, which):
        base, count = (CUT, 256 - CUT) if unit == "B" else (0, CUT)
        return base + which * (count // 2), count // 2

    def full_rows(unit):
        return (CUT, 256 - CUT) if unit == "B" else (0, CUT)

    def y_of(unit):
        return y if unit == "B" else y + (0, -1, 1, 2)[unit]

    def dyn_block(hh, yy, base, count):
        return wfull.at[mod(hh, 4) * 4 + mod(yy, 4), c, pl.ds(pl.multiple_of(base, 16), count)]

    def spread_b(tag, hh, base, count):
        ref = dyn_block(hh, y, base, count)
        for d in deltas:
            send(("by", tag, d), ref, ref, d_y[d])

    def got_b(tag, hh, base, count):
        for d in deltas:
            got(("by", tag, d))
            to_core(("by", tag, d), dyn_block(hh, y - d, base, count))

    def t0(unit):
        base, count = full_rows(unit)
        if unit in (1, 2, 3):
            d = deltas[unit - 1]
            got(("ay", d))
            to_core(("ay", d), wblock(h, y - d, 0, CUT))
        ref = wblock(h, y_of(unit), base, count)
        send(("o1", unit), ref, ref, d_out)
        if unit == "B":
            spread_b("own", h, base, count)

    def t1(unit):
        base, count = full_rows(unit)
        got(("o1", unit))
        ref = wblock(h + sgn, y_of(unit), base, count)
        send(("m1", unit), ref, ref, d_mate)
        to_core(("o1", unit), ref)
        if unit == "B":
            spread_b("out", h + sgn, base, count)

    def t2(unit):
        base, count = full_rows(unit)
        got(("m1", unit))
        ref = wblock(h - sgn, y_of(unit), base, count)
        first, size = half_rows(unit, 1 - lo)
        part_ref = dyn_block(h - sgn, y_of(unit), first, size)
        send(("o2", unit), part_ref, part_ref, d_out)
        to_core(("m1", unit), ref)
        if unit == "B":
            spread_b("mate", h - sgn, base, count)

    def t3(unit):
        got(("o2", unit))
        first, size = half_rows(unit, lo)
        ref = dyn_block(h + 2, y_of(unit), first, size)
        send(("m2", unit), ref, ref, d_mate)
        to_core(("o2", unit), ref)
        if unit == "B":
            spread_b("far1", h + 2, first, size)

    def t4(unit):
        got(("m2", unit))
        first, size = half_rows(unit, 1 - lo)
        ref = dyn_block(h + 2, y_of(unit), first, size)
        to_core(("m2", unit), ref)
        if unit == "B":
            spread_b("far2", h + 2, first, size)

    def start_gather():
        t0(0)
        t0("B")
        ref = wblock(h, y, 0, CUT)
        for d in deltas:
            send(("ay", d), ref, ref, d_y[d])

    at(6.0, start_gather)
    for unit, times in {
        0: (None, 11, 16, 19, 22),
        "B": (None, 12.5, 17.5, 20.5, 23.5),
        1: (12, 17, 22, 25, 28),
        2: (15, 22, 27, 30, 33),
        3: (18, 27, 32, 35, 38),
    }.items():
        for step, time in zip((t0, t1, t2, t3, t4), times):
            if time is not None:
                at(time, functools.partial(step, unit))
    bases = full_rows("B")
    at(20, lambda: got_b("own", h, *bases))
    at(22.4, lambda: got_b("out", h + sgn, *bases))
    at(24, lambda: got_b("mate", h - sgn, *bases))
    at(26, lambda: got_b("far1", h + 2, *half_rows("B", lo)))
    at(27, lambda: got_b("far2", h + 2, *half_rows("B", 1 - lo)))

    def own_norm():
        @pl.loop(0, 16)
        def _(jj):
            norm_block(2 * jj + c, nown, jj)

    at(6.5, own_norm)
    M = 256
    chunk_rows = 4 * R

    def products(m):
        if m == 0:
            got("cot")
        for g in range(4):
            if m == 0:
                got(("n", g))

            @pl.loop(0, 4)
            def _(yy, g=g):
                jj = 4 * g + yy
                rows = pl.ds(m * M, M)
                value = jnp.dot(cot_t[rows, :], nown[jj], preferred_element_type=F32)
                value += jnp.dot(cot_t_in[rows, :], nrecv[jj], preferred_element_type=F32)
                value = value.astype(BF16)
                for k in range(M // chunk_rows):
                    for q in range(4):
                        first = k * chunk_rows + q * R
                        part[m * (M // chunk_rows) + k, q, yy, g] = value[first : first + R]

    at(9.0, functools.partial(products, 0))
    at(11.0, functools.partial(products, 1))

    first_half, second_half = pl.ds(0, 2), pl.ds(2, 2)

    def x_first(k):
        x2, xr, xl = mod(x + 2, 4), mod(x + 1, 4), mod(x - 1, 4)
        send(("xa", 0, k), part.at[k, x2, first_half], xin_a.at[0, k], d_x[1])
        send(("xa", 1, k), part.at[k, x2, second_half], xin_a.at[1, k], d_x[-1])
        send(("xb", 0, k), part.at[k, xr, second_half], xin_b.at[0, k], d_x[1])
        send(("xb", 1, k), part.at[k, xl, first_half], xin_b.at[1, k], d_x[-1])

    def add_into(k, q, half, *others):
        @pl.loop(0, 2)
        def _(i):
            value = part[k, q, half * 2 + i].astype(F32)
            for other in others:
                value += other[i].astype(F32)
            part[k, q, half * 2 + i] = value.astype(BF16)

    def x_relay(k):
        xr, xl = mod(x + 1, 4), mod(x - 1, 4)
        got(("xa", 0, k))
        add_into(k, xr, 0, xin_a.at[0, k])
        send(("xc", 0, k), part.at[k, xr, first_half], xin_c.at[0, k], d_x[1])
        got(("xa", 1, k))
        add_into(k, xl, 1, xin_a.at[1, k])
        send(("xc", 1, k), part.at[k, xl, second_half], xin_c.at[1, k], d_x[-1])

    def x_last(k):
        got(("xb", 0, k))
        got(("xb", 1, k))
        got(("xc", 0, k))
        add_into(k, x, 0, xin_c.at[0, k], xin_b.at[1, k])
        got(("xc", 1, k))
        add_into(k, x, 1, xin_b.at[0, k], xin_c.at[1, k])
        for i, d in enumerate(deltas):
            send(("y", d, k), part.at[k, x, mod(y + d, 4)], yin.at[k, i], d_y[d])

    def y_last(k):
        for d in deltas:
            got(("y", d, k))
        value = part[k, x, y].astype(F32)
        for i in range(3):
            value += yin[k, i].astype(F32)
        value = value.astype(BF16)
        ts[k, 0] = value[:, :, :128]
        ts[k, 1] = value[:, :, 128:]
        for d in range(1, 8):
            z_to = mod(z + d, 8)
            send(("z", d, k), ts.at[k, lax.rem(z_to, 2), z_to // 2], zin.at[k, d - 1], d_z[d])

    def z_last(k):
        for d in range(1, 8):
            got(("z", d, k))
        value = ts[k, lo, h].astype(F32)
        for d in range(7):
            value += zin[k, d].astype(F32)
        wt[k, c, lo, x] = value.astype(BF16)
        ref = wt.at[k, c, lo, x]
        for d in deltas:
            send(("gx", d, k), ref, ref, d_x[d])

    d_diag = dev(z=z_mate, c=1 - c)

    def node_share(k):
        for d in deltas:
            got(("gx", d, k))
        ref = wt.at[k, c, lo]
        send(("gc", k), ref, ref, d_core)
        send(("gm", k), ref, ref, d_mate)
        send(("gd", k), ref, ref, d_diag)

    def write_block(k):
        for n in ("gc", "gm", "gd"):
            got((n, k))
        if (k + 1) * chunk_rows % SEQ == 0:
            first = (k + 1) * chunk_rows // SEQ - 1
            count = SEQ // chunk_rows
            for cc in range(2):
                for ll in range(2):
                    value = wt[pl.ds(first * count, count), cc, ll].astype(F32)
                    value = value.reshape(SEQ, 128)
                    wg_ref[pl.ds(cc * 256 + ll * 128, 128), pl.ds(first * SEQ, SEQ)] = value.T

    period = 36.0 / K
    for k in range(K):
        at(10.0 + max(0, k - 1) * period if k < K // 2 else max(11.5, 10 + (k - 1) * period),
           functools.partial(x_first, k))
        at(10.0 + (k + 0.8) * period, functools.partial(x_relay, k))
        done = 10.0 + (k + 1.2) * period
        at(done, functools.partial(x_last, k))
        at(done + 3, functools.partial(y_last, k))
        at(done + 6, functools.partial(z_last, k))
        at(done + 8, functools.partial(node_share, k))
        at(done + 10, functools.partial(write_block, k))

    acc_zero = []

    def row_grads(unit):
        if unit == 0:
            acc[...] = jnp.zeros_like(acc)
        while core_waits:
            name = core_waits.pop(0)
            got(name)
        yb = mod(y_of(unit), 4)

        @pl.loop(0, 8)
        def _(i):
            block = ((i // 2) * 4 + yb) * 2 + lax.rem(i, 2)
            lanes = pl.ds(pl.multiple_of(block * 256, 256), 256)
            ng = lax.dot_general(
                cot[...], wfull[(i // 2) * 4 + yb, lax.rem(i, 2)], (((1,), (1,)), ((), ())),
                preferred_element_type=F32)
            ngs[block] = ng
            both = ng * tok[:, lanes].astype(F32)
            gpart[pl.ds(block, 1), :] = jnp.sum(both * inverse(), axis=0, keepdims=True)
            both = both * gain_ref[pl.ds(block, 1), :]
            acc[...] += both[:, :128] + both[:, 128:]

    for unit, time in ((0, 28.5), (1, 30.5), (2, 34.5), (3, 40)):
        at(time, functools.partial(row_grads, unit))

    stores = []

    def finish_rows(quarter):
        inv = inverse()
        coef = inv * inv * inv * (jnp.sum(acc[...], axis=1, keepdims=True) / 8192.0)

        @pl.loop(0, 8)
        def _(i):
            block = quarter * 8 + i
            lanes = pl.ds(pl.multiple_of(block * 256, 256), 256)
            value = inv * (gain_ref[pl.ds(block, 1), :] * ngs[block]) - tok[:, lanes].astype(F32) * coef
            tok[:, lanes] = value.astype(BF16)

        lanes = pl.ds(quarter * 2048, 2048)
        copy = pltpu.make_async_copy(tok.at[:, lanes], ig_hbm.at[:, lanes], lsem.at[5 + quarter])
        copy.start()
        stores.append(copy)

    for quarter in range(4):
        at(41.5 + 0.5 * quarter, functools.partial(finish_rows, quarter))

    mine = pl.ds(pl.multiple_of(16 * c, 16), 16)

    def gain_core():
        send("g", gpart, gcore, d_core)

    def gain_x():
        got("g")
        gx[x] = gpart[mine, :] + gcore[mine, :]
        for d in deltas:
            send(("ggx", d), gx.at[x], gx.at[x], d_x[d])

    def gain_y():
        for d in deltas:
            got(("ggx", d))
        gy[y] = (gx[0] + gx[1]) + (gx[2] + gx[3])
        for d in deltas:
            send(("ggy", d), gy.at[y], gy.at[y], d_y[d])

    def gain_z():
        for d in deltas:
            got(("ggy", d))
        gz[z] = (gy[0] + gy[1]) + (gy[2] + gy[3])
        for d in range(1, 8):
            send(("ggz", d), gz.at[z], gz.at[z], d_z[d])

    def gain_last():
        for d in range(1, 8):
            got(("ggz", d))
        total = gz[0]
        for i in range(1, 8):
            total += gz[i]
        gg_ref[mine, :] = total
        send("gg", gg_ref.at[mine], gg_ref.at[mine], d_core)

    at(40.1, gain_core)
    at(42.1, gain_x)
    at(44.5, gain_y)
    at(47, gain_z)
    at(50, gain_last)
    at(59, lambda: got("gg"))

    for _, _, fn in sorted(events, key=lambda e: e[:2]):
        fn()
    for copy in sent:
        copy.wait_send()
    for copy in stores:
        copy.wait()


MESSAGES = 22 * K + 5 + 3 + 20 + 15 + 38 + 15


def on_device(
    tokens, norm_gain, value_weight, value_grads, new_logprobs, old_logprobs, advantages, lengths
):
    vmem = pl.BlockSpec(memory_space=pltpu.VMEM)
    smem = pl.BlockSpec(memory_space=pltpu.SMEM)
    hbm = pl.BlockSpec(memory_space=pl.ANY)
    input_grads, weight_grads, gain_grads = pl.pallas_call(
        kernel,
        out_shape=(
            jax.ShapeDtypeStruct((256, 8192), BF16),
            jax.ShapeDtypeStruct((512, 512), F32),
            jax.ShapeDtypeStruct((32, 256), F32),
        ),
        in_specs=[hbm, vmem, hbm, vmem, vmem, vmem, smem, smem],
        out_specs=(hbm, vmem, vmem),
        scratch_shapes=[
            pltpu.VMEM((256, 8192), BF16),
            pltpu.VMEM((16, 2, 256, 512), BF16),
            pltpu.VMEM((32, 256, 256), F32),
            pltpu.VMEM((16, 256, 256), BF16),
            pltpu.VMEM((16, 256, 256), BF16),
            pltpu.VMEM((16, 256, 256), BF16),
            pltpu.VMEM((256, 512), BF16),
            pltpu.VMEM((512, 256), BF16),
            pltpu.VMEM((512, 256), BF16),
            pltpu.VMEM((256, 128), F32),
            pltpu.VMEM((256, 128), F32),
            pltpu.VMEM((K, 4, 4, 4, R, 256), BF16),
            pltpu.VMEM((2, K, 2, 4, R, 256), BF16),
            pltpu.VMEM((2, K, 2, 4, R, 256), BF16),
            pltpu.VMEM((2, K, 2, 4, R, 256), BF16),
            pltpu.VMEM((K, 3, 4, R, 256), BF16),
            pltpu.VMEM((K, 2, 4, R, 128), BF16),
            pltpu.VMEM((K, 7, R, 128), BF16),
            pltpu.VMEM((K, 2, 2, 4, R, 128), BF16),
            pltpu.VMEM((32, 256), F32),
            pltpu.VMEM((32, 256), F32),
            pltpu.VMEM((4, 16, 256), F32),
            pltpu.VMEM((4, 16, 256), F32),
            pltpu.VMEM((8, 16, 256), F32),
            pltpu.SemaphoreType.DMA((9,)),
            pltpu.SemaphoreType.DMA((MESSAGES,)),
            pltpu.SemaphoreType.DMA((MESSAGES,)),
        ],
        compiler_params=pltpu.CompilerParams(
            collective_id=0, has_side_effects=True, vmem_limit_bytes=56 * 2**20
        ),
    )(
        tokens,
        norm_gain.reshape(32, 256),
        value_weight.reshape(2, 256, 512),
        value_grads,
        new_logprobs.reshape(2, SEQ),
        old_logprobs.reshape(2, SEQ),
        advantages,
        lengths,
    )
    return input_grads, weight_grads, gain_grads.reshape(8192)


def solution(mesh):
    rows = P(("node", "dp"))
    in_specs = (
        P(("node", "dp"), None), P(), P("dp", None), P(("node", "dp"), None), rows, rows, rows, rows,
    )
    out_specs = (P(("node", "dp"), None), P("dp", None), P())
    return jax.shard_map(
        on_device, mesh=mesh, in_specs=in_specs, out_specs=out_specs, check_vma=False
    )
```

time: 530 us -> 119 us (0.22)
  waiting for transfers between devices: 393 us -> 0 us
  Pallas kernels: 0 us -> 109 us
  blocking collectives: 75.7 us -> 0 us
  matrix products: 23.6 us -> 0 us
  between operations: 13.8 us -> 0.64 us
  other arithmetic: 7.48 us -> 0 us
    reduce_scatter x1 -> x0, waiting for transfers between devices: 229 us -> none  [on_device(): lax.psum_scatter(jnp.einsum('rd,rv->dv', normed, value_cotan, preferred_e...]
    all_gather x1 -> x0, waiting for transfers between devices: 114 us -> none  [on_device(): full_weight = lax.all_gather(value_weight, 'dp', axis=0, tiled=True)]
    pallas_call x0 -> x1, Pallas kernels: none -> 109 us  [on_device(): pl.pallas_call(kernel, out_shape=(jax.ShapeDtypeStruct((256, 8192), BF16)...]
    psum x1 -> x0, blocking collectives: 75.7 us -> none  [on_device(): gain_total = lax.psum(gain_local, ('node', 'dp'))]
    psum x1 -> x0, waiting for transfers between devices: 49.2 us -> none  [on_device(): weight_total = lax.psum(local_sum, 'node')]
    dot_general x3 -> x0, matrix products: 23.6 us -> none  [the longest x2 13.4 us: block_terms(): lax.dot_general(cotan_block, full_weight, (((1,), (1,)), ((), ())), prefe...]
    dynamic_update_slice x8 -> x0, local copies, waits for them, and re-layouts: 7.92 us -> none  [on_device(): lax.map(each_block, (tokens.reshape(block_count, BLOCK, feature_count), v...]
  transfers between devices with their start and end apart: 3 -> 0, of which waited for: 3 -> 0; matrix products, arithmetic and copies ran while one was open for 1% -> 0% of each run, Pallas kernels for 0% -> 0%
where the time goes in v1:
time: 119 us; the launch traced here: 118 us
  Pallas kernels  109 us (92%)
  local copies, waits for them, and re-layouts  8.47 us (7%)
    pallas_call x1, Pallas kernels, on_device(): pl.pallas_call(kernel, out_shape=(jax.ShapeDtypeStruct((256, 8192), BF16)...  109 us
    unnamed x5, local copies, waits for them, and re-layouts  7.09 us

profile of v1, /device:TPU:1, one launch (start us, length us, event | category | flops | bytes accessed | tf_op | source)
XLA Modules:
  0.0 118.4 jit_solution(6709467532870639800)
XLA Ops:
  0.6 1.4 %reshape.21.gain_ref = f32[32,256]{1,0:T(8,128)} reshape(f32[8192]{0:T(1024)} %param.9) | data formatting | bytes 65536 | tf_op jit(solution)/shard_map/reshape | solution.py:522
  2.0 109.3 %shard_map.103 = (bf16[256,8192]{1,0:T(8,128)(2,1)}, f32[512,512]{1,0:T(8,128)}, f32[32,256]{1,0:T(8,128)}) custom-call(bf16[256,8192]{1,0:T(8,128)(2,1)} %tok_hbm.1, f32[32,256]{1,0:T(8,128)} %reshape.21.gain_ref, bf16[2,256,512]{2,1,0:T(8,128)(2,1)} %bitcast.5, bf16[256,512]{1,0:T(8,128)(2,1)} %vg_ref.1, f32[2,128]{1,0:T(2,128)} %bitcast.8, ...), custom_call_target="tpu_custom_call" | custom-call | tf_op jit(solution)/shard_map/pallas_call | solution.py:479
  111.3 1.4 %copy.11 = f32[4,2,8,128]{3,1,2,0:T(2,128)} copy(f32[4,2,8,128]{3,2,1,0:T(8,128)} %bitcast.7) | data formatting | bytes 65536
  112.7 0.0 copy-start
  112.7 4.7 %copy.14 = bf16[256,8192]{1,0:T(8,128)(2,1)} copy(bf16[256,8192]{1,0:T(8,128)(2,1)} %get-tuple-element.12) | data formatting | bytes 8388608
  117.4 0.0 copy-done
  117.4 1.0 copy.15
Async XLA Ops:
  112.7 4.7 %copy-start = (f32[512,512]{1,0:T(8,128)S(1)}, f32[512,512]{1,0:T(8,128)}, u32[]{:S(2)}) copy-start(f32[512,512]{1,0:T(8,128)} %get-tuple-element.13) | copy-start | bytes 3145732

commit v2 on v1

v2 whole, which is shorter than its diff:
```python
import functools

import jax
import jax.numpy as jnp
from jax import lax
from jax.experimental import pallas as pl
from jax.experimental.pallas import tpu as pltpu
from jax.sharding import PartitionSpec as P

SEQ = 128
EPS = 1e-06
K = 8
R = 128 // K
YF = ()
FAST = 2
CUT = 160
ORDER = (
    ("t0", 0, 0), ("t0", 0, 1), ("t0", 4, "b"), ("p", 0, 0), ("p", 0, 1), ("p", 0, 2), ("t0", 1, 0),
    ("t0", 2, 0), ("t1", 0, 0), ("p", 0, 3), ("xf", 0), ("xf", 1), ("p", 1, 0), ("p", 1, 1), ("t1", 0, 1),
    ("p", 1, 2), ("t0", 3, 0), ("p", 1, 3), ("t0", 1, 1), ("t0", 2, 1), ("t1", 4, "b"), ("t2", 0, 0),
    ("xr", 0, 0), ("xr", 1, 0), ("xf", 2), ("t1", 1, 0), ("t0", 3, 1), ("t2", 0, 1), ("t1", 2, 0),
    ("xr", 0, 1), ("xr", 1, 1), ("xf", 3), ("t1", 3, 0), ("t2", 4, "b"), ("b", 0), ("xl", 0), ("t1", 1, 1),
    ("t2", 1, 0), ("xr", 0, 2), ("xr", 1, 2), ("xf", 4), ("t1", 2, 1), ("t2", 2, 0), ("b", 1), ("t1", 3, 1),
    ("t2", 3, 0), ("xl", 1), ("xr", 0, 3), ("xr", 1, 3), ("xf", 5), ("t3", 0), ("t2", 1, 1), ("t3", 4),
    ("t2", 2, 1), ("b", 2), ("xl", 2), ("t2", 3, 1), ("yl", 0), ("xr", 0, 4), ("xr", 1, 4), ("xf", 6),
    ("t3", 1), ("yl", 1), ("t4", 0), ("t4", 4), ("t3", 2), ("xl", 3), ("b", 3), ("rg", 0), ("xr", 0, 5),
    ("xr", 1, 5), ("t3", 3), ("xf", 7), ("t4", 1), ("yl", 2), ("zl", 0), ("xl", 4), ("b", 4), ("zl", 1),
    ("t4", 2), ("xr", 0, 6), ("xr", 1, 6), ("yl", 3), ("rg", 1), ("t4", 3), ("rg", 2), ("xl", 5),
    ("xr", 0, 7), ("xr", 1, 7), ("yl", 4), ("zl", 2), ("zl", 3), ("ns", 0), ("ns", 1), ("rg", 3), ("g", 0),
    ("xl", 6), ("fr", 0), ("xl", 7), ("g", 1), ("yl", 5), ("wr", 0), ("wr", 1), ("zl", 4), ("ns", 2),
    ("ns", 3), ("fr", 1), ("fr", 2), ("fr", 3), ("yl", 6), ("g", 2), ("yl", 7), ("ns", 4), ("wr", 2),
    ("zl", 5), ("wr", 3), ("g", 3), ("ns", 5), ("zl", 6), ("wr", 4), ("zl", 7), ("g", 4), ("wr", 5),
    ("wr", 6), ("wr", 7), ("g", 5),
)
MESH = pl.DeviceIdType.MESH
F32 = jnp.float32
BF16 = jnp.bfloat16


def mod(a, n):
    return lax.rem(a + 2 * n, n)


def kernel(
    tok_hbm, gain_ref, w_hbm, vg_ref, new_ref, old_ref, adv_ref, len_ref,
    ig_hbm, wg_ref, gg_ref,
    tok, wfull, ngs, nown, nsend, nrecv, cot, cot_t, cot_t_in, inv_ref, acc,
    part, xin_a, xin_b, xin_c, yin, ts, zin, wt, yf_in, xd_in, tsf, zinf,
    gpart, gcore, gx, gy, gz,
    lsem, ssem, rsem,
):
    node = lax.axis_index("node")
    dp = lax.axis_index("dp")
    c = lax.rem(node, 2)
    x = lax.rem(node // 2, 4)
    lo = node // 8
    h = dp // 4
    y = lax.rem(dp, 4)
    z = 2 * h + lo
    j_me = dp

    def dev(x=x, y=y, z=z, c=c):
        return (lax.rem(z, 2) * 8 + x * 2 + c, (z // 2) * 4 + y)

    sgn = 2 * lo - 1
    z_out = mod(z + sgn, 8)
    z_mate = mod(z - sgn, 8)
    d_core = dev(c=1 - c)
    d_x = {1: dev(x=mod(x + 1, 4)), -1: dev(x=mod(x - 1, 4)), 2: dev(x=mod(x + 2, 4))}
    d_y = {1: dev(y=mod(y + 1, 4)), -1: dev(y=mod(y - 1, 4)), 2: dev(y=mod(y + 2, 4))}
    d_out = dev(z=z_out)
    d_mate = dev(z=z_mate)
    d_z = {d: dev(z=mod(z + d, 8)) for d in range(1, 8)}

    d_diag = dev(z=z_mate, c=1 - c)
    d_xf = {d: dev(x=mod(x + d, 4), c=1 - c) for d in (1, -1, 2)}

    barrier = pltpu.get_barrier_semaphore()
    peers = [d_core, *d_x.values(), *d_xf.values(), *d_y.values(), *d_z.values(), d_diag]
    for peer in peers:
        pl.semaphore_signal(barrier, inc=1, device_id=peer, device_id_type=MESH)

    loads = []
    for r in range(4):
        loads.append(pltpu.make_async_copy(
            tok_hbm.at[pl.ds(r * 64, 64)], tok.at[pl.ds(r * 64, 64)], lsem.at[r]))
    wload = pltpu.make_async_copy(w_hbm, wfull.at[j_me], lsem.at[4])
    for cp in loads:
        cp.start()
    wload.start()

    names = {}
    sent = []

    def message(name, src, dst, device):
        index = names.setdefault(name, len(names))
        return pltpu.make_async_remote_copy(
            src_ref=src, dst_ref=dst, send_sem=ssem.at[index], recv_sem=rsem.at[index],
            device_id=device, device_id_type=MESH)

    waits = {}

    def send(name, src, dst, device):
        copy = message(name, src, dst, device)
        copy.start()
        sent.append(copy)
        waits[name] = copy

    def got(name):
        waits.pop(name).wait_recv()

    row = lax.broadcasted_iota(jnp.int32, (2, SEQ), 0)
    pos = lax.broadcasted_iota(jnp.int32, (2, SEQ), 1)
    adv = jnp.where(row == 0, adv_ref[0], adv_ref[1])
    length = jnp.where(row == 0, len_ref[0], len_ref[1])
    alive = (pos < length).astype(F32)
    ratio = jnp.exp(new_ref[...] - old_ref[...])
    weight = -adv * jnp.clip(ratio, 0.8, 1.2) / SEQ * alive
    eye = lax.broadcasted_iota(jnp.int32, (SEQ, SEQ), 0) == lax.broadcasted_iota(
        jnp.int32, (SEQ, SEQ), 1)
    for s in range(2):
        column = jnp.sum(jnp.where(eye, weight[s : s + 1, :], 0.0), axis=1, keepdims=True)
        wide = column * vg_ref[pl.ds(s * SEQ, SEQ), :].astype(F32)
        cot[pl.ds(s * SEQ, SEQ), :] = wide.astype(BF16)
        cot_t[:, pl.ds(s * SEQ, SEQ)] = wide.T.astype(BF16)

    for r in range(4):
        loads[r].wait()
        rows = pl.ds(r * 64, 64)

        def squares(i, total):
            part_ = tok[rows, pl.ds(pl.multiple_of(i * 512, 512), 512)].astype(F32)
            part_ = part_ * part_
            return total + ((part_[:, :128] + part_[:, 128:256])
                            + (part_[:, 256:384] + part_[:, 384:]))

        total = lax.fori_loop(0, 16, squares, jnp.zeros((64, 128), F32), unroll=2)
        mean = jnp.sum(total, axis=1, keepdims=True) / 8192.0
        inv_ref[rows, :] = jnp.broadcast_to(lax.rsqrt(mean + EPS), (64, 128))

    def inverse():
        return inv_ref[:, 0:1]

    def gain_row(block):
        return jnp.concatenate([gain_ref[pl.ds(2 * block, 1), :], gain_ref[pl.ds(2 * block + 1, 1), :]], axis=1)

    def norm_block(block, dst, jj):
        lanes = pl.ds(pl.multiple_of(block * 256, 256), 256)
        value = tok[:, lanes].astype(F32) * inverse() * gain_row(block)
        dst[jj] = value.astype(BF16)

    @pl.loop(0, 16)
    def _(jj):
        norm_block(2 * jj + (1 - c), nsend, jj)

    @pl.loop(0, 16)
    def _(jj):
        norm_block(2 * jj + c, nown, jj)

    wload.wait()
    pl.semaphore_wait(barrier, len(peers))

    events = {}

    def piece(name, fn, *args):
        events[name] = functools.partial(fn, *args)

    send("cot", cot_t, cot_t_in, d_core)
    for g in range(4):
        send(("n", g), nsend.at[pl.ds(4 * g, 4)], nrecv.at[pl.ds(4 * g, 4)], d_core)

    deltas = (1, -1, 2)

    from_core = {0: [], 1: [], 2: [], 3: []}

    def to_core(name, ref, group):
        send(("k", name), ref, ref, d_core)
        from_core[group].append(("k", name))

    def rows_of(unit):
        if unit[1] == "b":
            return CUT, 256 - CUT
        return unit[1] * (CUT // 2), CUT // 2

    def half_rows(u, which):
        if u == 4:
            return CUT + which * ((256 - CUT) // 2), (256 - CUT) // 2
        return which * (CUT // 2), CUT // 2

    def y_of(u):
        return y + (0, -1, 1, 2, 0)[u]

    def block_rows(hh, yy, base, count):
        return wfull.at[mod(hh, 4) * 4 + mod(yy, 4), c, pl.ds(pl.multiple_of(base, 16), count)]

    def group_of(u):
        return u % 4

    def spread_b(tag, hh, base, count):
        ref = block_rows(hh, y, base, count)
        for d in deltas:
            send(("by", tag, d), ref, ref, d_y[d])

    def got_b(tag, hh, base, count):
        for i, d in enumerate(deltas):
            got(("by", tag, d))
            to_core(("by", tag, d), block_rows(hh, y - d, base, count), i + 1)

    def t0(unit):
        u, s = unit
        base, count = rows_of(unit)
        if u in (1, 2, 3):
            d = deltas[u - 1]
            got(("ay", d, s))
            to_core(("ay", d, s), block_rows(h, y - d, base, count), u)
        ref = block_rows(h, y_of(u), base, count)
        send(("o1", unit), ref, ref, d_out)
        if u == 4:
            spread_b("own", h, base, count)
        elif u == 0:
            for d in deltas:
                send(("ay", d, s), ref, ref, d_y[d])

    def t1(unit):
        u = unit[0]
        base, count = rows_of(unit)
        got(("o1", unit))
        ref = block_rows(h + sgn, y_of(u), base, count)
        send(("m1", unit), ref, ref, d_mate)
        to_core(("o1", unit), ref, group_of(u))
        if u == 4:
            spread_b("out", h + sgn, base, count)

    def t2(unit):
        u, s = unit
        base, count = rows_of(unit)
        got(("m1", unit))
        ref = block_rows(h - sgn, y_of(u), base, count)
        if s != 0:
            half = block_rows(h - sgn, y_of(u), *half_rows(u, 1 - lo))
            send(("o2", u), half, half, d_out)
        to_core(("m1", unit), ref, group_of(u))
        if u == 4:
            spread_b("mate", h - sgn, base, count)

    def t3(u):
        got(("o2", u))
        first, size = half_rows(u, lo)
        ref = block_rows(h + 2, y_of(u), first, size)
        send(("m2", u), ref, ref, d_mate)
        to_core(("o2", u), ref, group_of(u))
        if u == 4:
            spread_b("far1", h + 2, first, size)

    def t4(u):
        got(("m2", u))
        first, size = half_rows(u, 1 - lo)
        ref = block_rows(h + 2, y_of(u), first, size)
        to_core(("m2", u), ref, group_of(u))
        if u == 4:
            spread_b("far2", h + 2, first, size)

    for u in range(5):
        for s in ((0, 1) if u < 4 else ("b",)):
            piece(("t0", u, s), t0, (u, s))
            piece(("t1", u, s), t1, (u, s))
            piece(("t2", u, s), t2, (u, s))
        piece(("t3", u), t3, u)
        piece(("t4", u), t4, u)
    b_rows = rows_of((4, "b"))
    piece(("b", 0), got_b, "own", h, *b_rows)
    piece(("b", 1), got_b, "out", h + sgn, *b_rows)
    piece(("b", 2), got_b, "mate", h - sgn, *b_rows)
    piece(("b", 3), got_b, "far1", h + 2, *half_rows(4, lo))
    piece(("b", 4), got_b, "far2", h + 2, *half_rows(4, 1 - lo))

    M = 256
    chunk_rows = 4 * R

    def products(m, g):
        if (m, g) == (0, 0):
            got("cot")
        if m == 0:
            got(("n", g))

        @pl.loop(0, 4)
        def _(yy):
            jj = 4 * g + yy
            rows = pl.ds(m * M, M)
            value = jnp.dot(cot_t[rows, :], nown[jj], preferred_element_type=F32)
            value += jnp.dot(cot_t_in[rows, :], nrecv[jj], preferred_element_type=F32)
            value = value.astype(BF16)
            for k in range(M // chunk_rows):
                for q in range(4):
                    first = k * chunk_rows + q * R
                    part[m * (M // chunk_rows) + k, q, yy, g] = value[first : first + R]

    for m in range(2):
        for g in range(4):
            piece(("p", m, g), products, m, g)

    first_half, second_half = pl.ds(0, 2), pl.ds(2, 2)

    def x_first(k):
        x2, xr, xl = mod(x + 2, 4), mod(x + 1, 4), mod(x - 1, 4)
        send(("xa", 0, k), part.at[k, x2, first_half], xin_a.at[0, k], d_x[1])
        send(("xa", 1, k), part.at[k, x2, second_half], xin_a.at[1, k], d_x[-1])
        send(("xb", 0, k), part.at[k, xr, second_half], xin_b.at[0, k], d_x[1])
        send(("xb", 1, k), part.at[k, xl, first_half], xin_b.at[1, k], d_x[-1])

    def add_into(k, q, half, *others):
        @pl.loop(0, 2)
        def _(i):
            value = part[k, q, half * 2 + i].astype(F32)
            for other in others:
                value += other[i].astype(F32)
            part[k, q, half * 2 + i] = value.astype(BF16)

    def x_relay(way, k):
        q = mod(x + (1, -1)[way], 4)
        got(("xa", way, k))
        add_into(k, q, way, xin_a.at[way, k])
        half = (first_half, second_half)[way]
        send(("xc", way, k), part.at[k, q, half], xin_c.at[way, k], d_x[(1, -1)[way]])

    def x_last(k):
        for way in range(2):
            got(("xb", 1 - way, k))
            got(("xc", way, k))
            add_into(k, x, way, xin_c.at[way, k], xin_b.at[1 - way, k])
        for i, d in enumerate(deltas):
            send(("y", d, k), part.at[k, x, mod(y + d, 4)], yin.at[k, i], d_y[d])

    def y_last(k):
        for d in deltas:
            got(("y", d, k))
        value = part[k, x, y].astype(F32)
        for i in range(3):
            value += yin[k, i].astype(F32)
        z_first(k, value.astype(BF16))

    def z_first(k, value):
        fast = k - (K - FAST)
        if fast >= 0:
            tsf[fast] = value
            zinf[fast, z] = tsf[fast, h]
            for d in range(1, 8):
                send(("z", d, k), tsf.at[fast, mod(z + d, 8) // 2], zinf.at[fast, z], d_z[d])
            return
        ts[k, 0] = value[:, :, :128]
        ts[k, 1] = value[:, :, 128:]
        for d in range(1, 8):
            z_to = mod(z + d, 8)
            send(("z", d, k), ts.at[k, lax.rem(z_to, 2), z_to // 2], zin.at[k, d - 1], d_z[d])

    def y_first(k):
        n = YF.index(k)
        for i, d in enumerate(deltas):
            send(("yf", d, k), part.at[k, pl.ds(0, 4), mod(y + d, 4)], yf_in.at[n, i], d_y[d])

    def y_middle(k):
        n = YF.index(k)
        for d in deltas:
            got(("yf", d, k))

        @pl.loop(0, 4)
        def _(q):
            value = part[k, q, y].astype(F32)
            for i in range(3):
                value += yf_in[n, i, q].astype(F32)
            part[k, q, y] = value.astype(BF16)

        for i, d in enumerate(deltas):
            send(("xd", d, k), part.at[k, mod(x + d, 4), y], xd_in.at[n, i], d_x[d])

    def x_direct_last(k):
        n = YF.index(k)
        for d in deltas:
            got(("xd", d, k))
        value = part[k, x, y].astype(F32)
        for i in range(3):
            value += xd_in[n, i].astype(F32)
        z_first(k, value.astype(BF16))

    def z_last(k):
        for d in range(1, 8):
            got(("z", d, k))
        fast = k - (K - FAST)
        if fast >= 0:
            value = zinf[fast, 0].astype(F32)
            for i in range(1, 8):
                value += zinf[fast, i].astype(F32)
            value = value.astype(BF16)
            wt[k, c, 0, x] = value[:, :128]
            wt[k, c, 1, x] = value[:, 128:]
            ref = wt.at[k, c, pl.ds(0, 2), x]
            send(("gf", 0, k), ref, ref, d_core)
            for d in deltas:
                send(("gf", d, k), ref, ref, d_x[d])
                send(("gg", d, k), ref, ref, d_xf[d])
            return
        value = ts[k, lo, h].astype(F32)
        for d in range(7):
            value += zin[k, d].astype(F32)
        wt[k, c, lo, x] = value.astype(BF16)
        ref = wt.at[k, c, lo, x]
        for d in deltas:
            send(("gx", d, k), ref, ref, d_x[d])

    def node_share(k):
        for d in deltas:
            got(("gx", d, k))
        ref = wt.at[k, c, lo]
        send(("gc", k), ref, ref, d_core)
        send(("gm", k), ref, ref, d_mate)
        send(("gd", k), ref, ref, d_diag)

    def write_block(k):
        if k >= K - FAST:
            got(("gf", 0, k))
            for d in deltas:
                got(("gf", d, k))
                got(("gg", d, k))
        else:
            for n in ("gc", "gm", "gd"):
                got((n, k))
        if (k + 1) * chunk_rows % SEQ == 0:
            first = (k + 1) * chunk_rows // SEQ - 1
            count = SEQ // chunk_rows
            for cc in range(2):
                for ll in range(2):
                    value = wt[pl.ds(first * count, count), cc, ll].astype(F32)
                    value = value.reshape(SEQ, 128)
                    wg_ref[pl.ds(cc * 256 + ll * 128, 128), pl.ds(first * SEQ, SEQ)] = value.T

    for k in range(K):
        if k in YF:
            piece(("yf", k), y_first, k)
            piece(("ym", k), y_middle, k)
            piece(("xd", k), x_direct_last, k)
        else:
            piece(("xf", k), x_first, k)
            piece(("xr", 0, k), x_relay, 0, k)
            piece(("xr", 1, k), x_relay, 1, k)
            piece(("xl", k), x_last, k)
            piece(("yl", k), y_last, k)
        piece(("zl", k), z_last, k)
        if k < K - FAST:
            piece(("ns", k), node_share, k)
        piece(("wr", k), write_block, k)

    acc[...] = jnp.zeros_like(acc)

    def row_grads(group):
        for name in from_core[group]:
            got(name)
        yb = mod(y_of(group), 4)

        @pl.loop(0, 8)
        def _(i):
            block = ((i // 2) * 4 + yb) * 2 + lax.rem(i, 2)
            lanes = pl.ds(pl.multiple_of(block * 256, 256), 256)
            ng = lax.dot_general(
                cot[...], wfull[(i // 2) * 4 + yb, lax.rem(i, 2)], (((1,), (1,)), ((), ())),
                preferred_element_type=F32)
            ngs[block] = ng
            both = ng * tok[:, lanes].astype(F32)
            sums = jnp.sum(both * inverse(), axis=0, keepdims=True)
            gpart[pl.ds(2 * block, 1), :] = sums[:, :128]
            gpart[pl.ds(2 * block + 1, 1), :] = sums[:, 128:]
            both = both * gain_row(block)
            acc[...] += both[:, :128] + both[:, 128:]

    for group in range(4):
        piece(("rg", group), row_grads, group)

    stores = []

    def finish_rows(quarter):
        inv = inverse()
        coef = inv * inv * inv * (jnp.sum(acc[...], axis=1, keepdims=True) / 8192.0)

        @pl.loop(0, 8)
        def _(i):
            block = quarter * 8 + i
            lanes = pl.ds(pl.multiple_of(block * 256, 256), 256)
            value = inv * (gain_row(block) * ngs[block]) - tok[:, lanes].astype(F32) * coef
            tok[:, lanes] = value.astype(BF16)

        lanes = pl.ds(quarter * 2048, 2048)
        copy = pltpu.make_async_copy(tok.at[:, lanes], ig_hbm.at[:, lanes], lsem.at[5 + quarter])
        copy.start()
        stores.append(copy)

    for quarter in range(4):
        piece(("fr", quarter), finish_rows, quarter)

    mine = pl.ds(pl.multiple_of(32 * c, 32), 32)

    def gain_core():
        send("g", gpart, gcore, d_core)

    def gain_x():
        got("g")
        gx[x] = gpart[mine, :] + gcore[mine, :]
        for d in deltas:
            send(("ggx", d), gx.at[x], gx.at[x], d_x[d])

    def gain_y():
        for d in deltas:
            got(("ggx", d))
        gy[y] = (gx[0] + gx[1]) + (gx[2] + gx[3])
        for d in deltas:
            send(("ggy", d), gy.at[y], gy.at[y], d_y[d])

    def gain_z():
        for d in deltas:
            got(("ggy", d))
        gz[z] = (gy[0] + gy[1]) + (gy[2] + gy[3])
        for d in range(1, 8):
            send(("ggz", d), gz.at[z], gz.at[z], d_z[d])

    def gain_last():
        for d in range(1, 8):
            got(("ggz", d))
        total = gz[0]
        for i in range(1, 8):
            total += gz[i]
        gg_ref[mine, :] = total
        send("gg", gg_ref.at[mine], gg_ref.at[mine], d_core)

    for i, fn in enumerate((gain_core, gain_x, gain_y, gain_z, gain_last)):
        piece(("g", i), fn)
    piece(("g", 5), got, "gg")

    for name in ORDER:
        events.pop(name)()
    assert not events and not waits
    for copy in sent:
        copy.wait_send()
    for copy in stores:
        copy.wait()


MESSAGES = 296


def on_device(
    tokens, norm_gain, value_weight, value_grads, new_logprobs, old_logprobs, advantages, lengths
):
    vmem = pl.BlockSpec(memory_space=pltpu.VMEM)
    smem = pl.BlockSpec(memory_space=pltpu.SMEM)
    hbm = pl.BlockSpec(memory_space=pl.ANY)
    input_grads, weight_grads, gain_grads = pl.pallas_call(
        kernel,
        out_shape=(
            jax.ShapeDtypeStruct((256, 8192), BF16),
            jax.ShapeDtypeStruct((512, 512), F32),
            jax.ShapeDtypeStruct((64, 128), F32),
        ),
        in_specs=[hbm, vmem, hbm, vmem, vmem, vmem, smem, smem],
        out_specs=(hbm, vmem, vmem),
        scratch_shapes=[
            pltpu.VMEM((256, 8192), BF16),
            pltpu.VMEM((16, 2, 256, 512), BF16),
            pltpu.VMEM((32, 256, 256), F32),
            pltpu.VMEM((16, 256, 256), BF16),
            pltpu.VMEM((16, 256, 256), BF16),
            pltpu.VMEM((16, 256, 256), BF16),
            pltpu.VMEM((256, 512), BF16),
            pltpu.VMEM((512, 256), BF16),
            pltpu.VMEM((512, 256), BF16),
            pltpu.VMEM((256, 128), F32),
            pltpu.VMEM((256, 128), F32),
            pltpu.VMEM((K, 4, 4, 4, R, 256), BF16),
            pltpu.VMEM((2, K, 2, 4, R, 256), BF16),
            pltpu.VMEM((2, K, 2, 4, R, 256), BF16),
            pltpu.VMEM((2, K, 2, 4, R, 256), BF16),
            pltpu.VMEM((K, 3, 4, R, 256), BF16),
            pltpu.VMEM((K, 2, 4, R, 128), BF16),
            pltpu.VMEM((K, 7, R, 128), BF16),
            pltpu.VMEM((K, 2, 2, 4, R, 128), BF16),
            pltpu.VMEM((max(len(YF), 1), 3, 4, 4, R, 256), BF16),
            pltpu.VMEM((max(len(YF), 1), 3, 4, R, 256), BF16),
            pltpu.VMEM((max(FAST, 1), 4, R, 256), BF16),
            pltpu.VMEM((max(FAST, 1), 8, R, 256), BF16),
            pltpu.VMEM((64, 128), F32),
            pltpu.VMEM((64, 128), F32),
            pltpu.VMEM((4, 32, 128), F32),
            pltpu.VMEM((4, 32, 128), F32),
            pltpu.VMEM((8, 32, 128), F32),
            pltpu.SemaphoreType.DMA((9,)),
            pltpu.SemaphoreType.DMA((MESSAGES,)),
            pltpu.SemaphoreType.DMA((MESSAGES,)),
        ],
        compiler_params=pltpu.CompilerParams(
            collective_id=0, has_side_effects=True, vmem_limit_bytes=54 * 2**20
        ),
    )(
        tokens,
        norm_gain.reshape(64, 128),
        value_weight.reshape(2, 256, 512),
        value_grads,
        new_logprobs.reshape(2, SEQ),
        old_logprobs.reshape(2, SEQ),
        advantages,
        lengths,
    )
    return input_grads, weight_grads, gain_grads.reshape(8192)


def solution(mesh):
    rows = P(("node", "dp"))
    in_specs = (
        P(("node", "dp"), None), P(), P("dp", None), P(("node", "dp"), None), rows, rows, rows, rows,
    )
    out_specs = (P(("node", "dp"), None), P("dp", None), P())
    return jax.shard_map(
        on_device, mesh=mesh, in_specs=in_specs, out_specs=out_specs, check_vma=False
    )
```

time: 119 us -> 88 us (0.74)
  Pallas kernels: 109 us -> 80.9 us
  local copies, waits for them, and re-layouts: 8.47 us -> 6.32 us
    pallas_call x1, Pallas kernels: 109 us -> 80.9 us  [on_device(): pl.pallas_call(kernel, out_shape=(jax.ShapeDtypeStruct((256, 8192), BF16)...]
    reshape x1 -> x0, local copies, waits for them, and re-layouts: 1.38 us -> none  [on_device(): norm_gain.reshape(32, 256)]
    unnamed x5 -> x7, local copies, waits for them, and re-layouts: 7.09 us -> 6.32 us
where the time goes in v2:
time: 88 us; the launch traced here: 87.9 us
  Pallas kernels  80.9 us (92%)
  local copies, waits for them, and re-layouts  6.32 us (7%)
    pallas_call x1, Pallas kernels, on_device(): pl.pallas_call(kernel, out_shape=(jax.ShapeDtypeStruct((256, 8192), BF16)...  80.9 us
    unnamed x7, local copies, waits for them, and re-layouts  6.32 us

profile of v2, /device:TPU:1, one launch (start us, length us, event | category | flops | bytes accessed | tf_op | source)
XLA Modules:
  0.0 87.9 jit_solution(13410592905622621791)
XLA Ops:
  0.6 80.9 %shard_map.103 = (bf16[256,8192]{1,0:T(8,128)(2,1)}, f32[512,512]{1,0:T(8,128)}, f32[64,128]{1,0:T(8,128)}) custom-call(bf16[256,8192]{1,0:T(8,128)(2,1)} %tok_hbm.1, f32[64,128]{1,0:T(8,128)} %bitcast.6, bf16[2,256,512]{2,1,0:T(8,128)(2,1)} %bitcast.5, bf16[256,512]{1,0:T(8,128)(2,1)} %vg_ref.1, f32[2,128]{1,0:T(2,128)} %bitcast.8, f32[2,128]{1,0:T(2,128)} %bitcast.9, ...), custom_call_target="tpu_custom_call" | custom-call | tf_op jit(solution)/shard_map/pallas_call | solution.py:554
  81.6 0.0 copy-start
  81.6 0.0 copy-start.1
  81.6 4.7 %copy.14 = bf16[256,8192]{1,0:T(8,128)(2,1)} copy(bf16[256,8192]{1,0:T(8,128)(2,1)} %get-tuple-element.12) | data formatting | bytes 8388608
  86.3 0.0 copy-done
  86.3 1.0 %copy.15 = f32[512,512]{1,0:T(8,128)} copy(f32[512,512]{1,0:T(8,128)S(1)} %copy-done) | data formatting | bytes 2097152
  87.3 0.0 copy-done.1
  87.3 0.6 copy.16
Async XLA Ops:
  81.6 4.7 %copy-start = (f32[512,512]{1,0:T(8,128)S(1)}, f32[512,512]{1,0:T(8,128)}, u32[]{:S(2)}) copy-start(f32[512,512]{1,0:T(8,128)} %get-tuple-element.13) | copy-start | bytes 3145732
  81.6 5.7 %copy-start.1 = (f32[64,128]{1,0:T(8,128)S(1)}, f32[64,128]{1,0:T(8,128)}, u32[]{:S(2)}) copy-start(f32[64,128]{1,0:T(8,128)} %get-tuple-element.8) | copy-start | bytes 98308

commit v3 on v2

--- a/solution.py
+++ b/solution.py
@@ -12,25 +12,25 @@
 K = 8
 R = 128 // K
 YF = ()
-FAST = 2
+FAST = 4
 CUT = 160
 ORDER = (
     ("t0", 0, 0), ("t0", 0, 1), ("t0", 4, "b"), ("p", 0, 0), ("p", 0, 1), ("p", 0, 2), ("t0", 1, 0),
     ("t0", 2, 0), ("t1", 0, 0), ("p", 0, 3), ("xf", 0), ("xf", 1), ("p", 1, 0), ("p", 1, 1), ("t1", 0, 1),
-    ("p", 1, 2), ("t0", 3, 0), ("p", 1, 3), ("t0", 1, 1), ("t0", 2, 1), ("t1", 4, "b"), ("t2", 0, 0),
-    ("xr", 0, 0), ("xr", 1, 0), ("xf", 2), ("t1", 1, 0), ("t0", 3, 1), ("t2", 0, 1), ("t1", 2, 0),
-    ("xr", 0, 1), ("xr", 1, 1), ("xf", 3), ("t1", 3, 0), ("t2", 4, "b"), ("b", 0), ("xl", 0), ("t1", 1, 1),
-    ("t2", 1, 0), ("xr", 0, 2), ("xr", 1, 2), ("xf", 4), ("t1", 2, 1), ("t2", 2, 0), ("b", 1), ("t1", 3, 1),
-    ("t2", 3, 0), ("xl", 1), ("xr", 0, 3), ("xr", 1, 3), ("xf", 5), ("t3", 0), ("t2", 1, 1), ("t3", 4),
+    ("p", 1, 2), ("p", 1, 3), ("t0", 3, 0), ("t0", 1, 1), ("t0", 2, 1), ("t1", 4, "b"), ("xr", 0, 0),
+    ("t2", 0, 0), ("xr", 1, 0), ("xf", 2), ("t1", 1, 0), ("t0", 3, 1), ("t2", 0, 1), ("xr", 0, 1),
+    ("xr", 1, 1), ("xf", 3), ("t1", 2, 0), ("t2", 4, "b"), ("t1", 3, 0), ("b", 0), ("xl", 0), ("t2", 1, 0),
+    ("t1", 1, 1), ("xr", 0, 2), ("xr", 1, 2), ("xf", 4), ("t1", 2, 1), ("t2", 2, 0), ("b", 1), ("t2", 3, 0),
+    ("t1", 3, 1), ("xl", 1), ("xr", 0, 3), ("xr", 1, 3), ("xf", 5), ("t2", 1, 1), ("t3", 0), ("t3", 4),
     ("t2", 2, 1), ("b", 2), ("xl", 2), ("t2", 3, 1), ("yl", 0), ("xr", 0, 4), ("xr", 1, 4), ("xf", 6),
-    ("t3", 1), ("yl", 1), ("t4", 0), ("t4", 4), ("t3", 2), ("xl", 3), ("b", 3), ("rg", 0), ("xr", 0, 5),
-    ("xr", 1, 5), ("t3", 3), ("xf", 7), ("t4", 1), ("yl", 2), ("zl", 0), ("xl", 4), ("b", 4), ("zl", 1),
-    ("t4", 2), ("xr", 0, 6), ("xr", 1, 6), ("yl", 3), ("rg", 1), ("t4", 3), ("rg", 2), ("xl", 5),
-    ("xr", 0, 7), ("xr", 1, 7), ("yl", 4), ("zl", 2), ("zl", 3), ("ns", 0), ("ns", 1), ("rg", 3), ("g", 0),
-    ("xl", 6), ("fr", 0), ("xl", 7), ("g", 1), ("yl", 5), ("wr", 0), ("wr", 1), ("zl", 4), ("ns", 2),
-    ("ns", 3), ("fr", 1), ("fr", 2), ("fr", 3), ("yl", 6), ("g", 2), ("yl", 7), ("ns", 4), ("wr", 2),
-    ("zl", 5), ("wr", 3), ("g", 3), ("ns", 5), ("zl", 6), ("wr", 4), ("zl", 7), ("g", 4), ("wr", 5),
-    ("wr", 6), ("wr", 7), ("g", 5),
+    ("t3", 1), ("t4", 0), ("yl", 1), ("t4", 4), ("xl", 3), ("t3", 2), ("b", 3), ("rg", 0), ("xr", 0, 5),
+    ("xr", 1, 5), ("xf", 7), ("t3", 3), ("yl", 2), ("t4", 1), ("zl", 0), ("xl", 4), ("b", 4), ("zl", 1),
+    ("xr", 0, 6), ("xr", 1, 6), ("t4", 2), ("rg", 1), ("t4", 3), ("rg", 2), ("xl", 5), ("zl", 2),
+    ("xr", 0, 7), ("xr", 1, 7), ("rg", 3), ("g", 0), ("ns", 0), ("ns", 1), ("yl", 3), ("xl", 6), ("g", 1),
+    ("ns", 2), ("yl", 4), ("xl", 7), ("yl", 5), ("wr", 0), ("fr", 0), ("wr", 1), ("fr", 1), ("g", 2),
+    ("fr", 2), ("wr", 2), ("yl", 6), ("zl", 3), ("yl", 7), ("zl", 4), ("fr", 3), ("g", 3), ("zl", 5),
+    ("ns", 3), ("zl", 6), ("zl", 7), ("g", 4), ("wr", 3), ("wr", 4), ("wr", 5), ("wr", 6), ("g", 5),
+    ("wr", 7),
 )
 MESH = pl.DeviceIdType.MESH
 F32 = jnp.float32
@@ -283,7 +283,7 @@
         if m == 0:
             got(("n", g))
 
-        @pl.loop(0, 4)
+        @pl.loop(0, 4, unroll=4)
         def _(yy):
             jj = 4 * g + yy
             rows = pl.ds(m * M, M)
@@ -309,7 +309,7 @@
         send(("xb", 1, k), part.at[k, xl, first_half], xin_b.at[1, k], d_x[-1])
 
     def add_into(k, q, half, *others):
-        @pl.loop(0, 2)
+        @pl.loop(0, 2, unroll=2)
         def _(i):
             value = part[k, q, half * 2 + i].astype(F32)
             for other in others:
@@ -456,7 +456,7 @@
             got(name)
         yb = mod(y_of(group), 4)
 
-        @pl.loop(0, 8)
+        @pl.loop(0, 8, unroll=4)
         def _(i):
             block = ((i // 2) * 4 + yb) * 2 + lax.rem(i, 2)
             lanes = pl.ds(pl.multiple_of(block * 256, 256), 256)
@@ -480,7 +480,7 @@
         inv = inverse()
         coef = inv * inv * inv * (jnp.sum(acc[...], axis=1, keepdims=True) / 8192.0)
 
-        @pl.loop(0, 8)
+        @pl.loop(0, 8, unroll=2)
         def _(i):
             block = quarter * 8 + i
             lanes = pl.ds(pl.multiple_of(block * 256, 256), 256)
@@ -542,7 +542,7 @@
         copy.wait()
 
 
-MESSAGES = 296
+MESSAGES = 298
 
 
 def on_device(

time: 88 us -> 85.3 us (0.969)
  Pallas kernels: 80.9 us -> 78.2 us
    pallas_call x1, Pallas kernels: 80.9 us -> 78.2 us  [on_device(): pl.pallas_call(kernel, out_shape=(jax.ShapeDtypeStruct((256, 8192), BF16)...]
where the time goes in v3:
time: 85.3 us; the launch traced here: 85.2 us
  Pallas kernels  78.2 us (92%)
  local copies, waits for them, and re-layouts  6.32 us (7%)
    pallas_call x1, Pallas kernels, on_device(): pl.pallas_call(kernel, out_shape=(jax.ShapeDtypeStruct((256, 8192), BF16)...  78.2 us
    unnamed x7, local copies, waits for them, and re-layouts  6.32 us

profile of v3, /device:TPU:1, one launch (start us, length us, event | category | flops | bytes accessed | tf_op | source)
XLA Modules:
  0.0 85.2 jit_solution(477746335388009653)
XLA Ops:
  0.6 78.2 %shard_map.103 = (bf16[256,8192]{1,0:T(8,128)(2,1)}, f32[512,512]{1,0:T(8,128)}, f32[64,128]{1,0:T(8,128)}) custom-call(bf16[256,8192]{1,0:T(8,128)(2,1)} %tok_hbm.1, f32[64,128]{1,0:T(8,128)} %bitcast.6, bf16[2,256,512]{2,1,0:T(8,128)(2,1)} %bitcast.5, bf16[256,512]{1,0:T(8,128)(2,1)} %vg_ref.1, f32[2,128]{1,0:T(2,128)} %bitcast.8, f32[2,128]{1,0:T(2,128)} %bitcast.9, ...), custom_call_target="tpu_custom_call" | custom-call | tf_op jit(solution)/shard_map/pallas_call | solution.py:554
  78.9 0.0 copy-start
  78.9 0.0 copy-start.1
  78.9 4.7 %copy.14 = bf16[256,8192]{1,0:T(8,128)(2,1)} copy(bf16[256,8192]{1,0:T(8,128)(2,1)} %get-tuple-element.12) | data formatting | bytes 8388608
  83.6 0.0 copy-done
  83.6 1.0 %copy.15 = f32[512,512]{1,0:T(8,128)} copy(f32[512,512]{1,0:T(8,128)S(1)} %copy-done) | data formatting | bytes 2097152
  84.6 0.0 copy-done.1
  84.6 0.6 copy.16
Async XLA Ops:
  78.9 4.7 %copy-start = (f32[512,512]{1,0:T(8,128)S(1)}, f32[512,512]{1,0:T(8,128)}, u32[]{:S(2)}) copy-start(f32[512,512]{1,0:T(8,128)} %get-tuple-element.13) | copy-start | bytes 3145732
  78.9 5.7 %copy-start.1 = (f32[64,128]{1,0:T(8,128)S(1)}, f32[64,128]{1,0:T(8,128)}, u32[]{:S(2)}) copy-start(f32[64,128]{1,0:T(8,128)} %get-tuple-element.8) | copy-start | bytes 98308

commit v4 on v3

--- a/solution.py
+++ b/solution.py
@@ -15,22 +15,22 @@
 FAST = 4
 CUT = 160
 ORDER = (
-    ("t0", 0, 0), ("t0", 0, 1), ("t0", 4, "b"), ("p", 0, 0), ("p", 0, 1), ("p", 0, 2), ("t0", 1, 0),
-    ("t0", 2, 0), ("t1", 0, 0), ("p", 0, 3), ("xf", 0), ("xf", 1), ("p", 1, 0), ("p", 1, 1), ("t1", 0, 1),
-    ("p", 1, 2), ("p", 1, 3), ("t0", 3, 0), ("t0", 1, 1), ("t0", 2, 1), ("t1", 4, "b"), ("xr", 0, 0),
-    ("t2", 0, 0), ("xr", 1, 0), ("xf", 2), ("t1", 1, 0), ("t0", 3, 1), ("t2", 0, 1), ("xr", 0, 1),
-    ("xr", 1, 1), ("xf", 3), ("t1", 2, 0), ("t2", 4, "b"), ("t1", 3, 0), ("b", 0), ("xl", 0), ("t2", 1, 0),
-    ("t1", 1, 1), ("xr", 0, 2), ("xr", 1, 2), ("xf", 4), ("t1", 2, 1), ("t2", 2, 0), ("b", 1), ("t2", 3, 0),
-    ("t1", 3, 1), ("xl", 1), ("xr", 0, 3), ("xr", 1, 3), ("xf", 5), ("t2", 1, 1), ("t3", 0), ("t3", 4),
-    ("t2", 2, 1), ("b", 2), ("xl", 2), ("t2", 3, 1), ("yl", 0), ("xr", 0, 4), ("xr", 1, 4), ("xf", 6),
-    ("t3", 1), ("t4", 0), ("yl", 1), ("t4", 4), ("xl", 3), ("t3", 2), ("b", 3), ("rg", 0), ("xr", 0, 5),
-    ("xr", 1, 5), ("xf", 7), ("t3", 3), ("yl", 2), ("t4", 1), ("zl", 0), ("xl", 4), ("b", 4), ("zl", 1),
-    ("xr", 0, 6), ("xr", 1, 6), ("t4", 2), ("rg", 1), ("t4", 3), ("rg", 2), ("xl", 5), ("zl", 2),
-    ("xr", 0, 7), ("xr", 1, 7), ("rg", 3), ("g", 0), ("ns", 0), ("ns", 1), ("yl", 3), ("xl", 6), ("g", 1),
-    ("ns", 2), ("yl", 4), ("xl", 7), ("yl", 5), ("wr", 0), ("fr", 0), ("wr", 1), ("fr", 1), ("g", 2),
-    ("fr", 2), ("wr", 2), ("yl", 6), ("zl", 3), ("yl", 7), ("zl", 4), ("fr", 3), ("g", 3), ("zl", 5),
-    ("ns", 3), ("zl", 6), ("zl", 7), ("g", 4), ("wr", 3), ("wr", 4), ("wr", 5), ("wr", 6), ("g", 5),
-    ("wr", 7),
+    ("t0", 0, 0), ("t0", 0, 1), ("t0", 4, "b"), ("p", 0, 0), ("xg", 0), ("p", 0, 1), ("xg", 1), ("p", 0, 2),
+    ("xg", 2), ("t0", 1, 0), ("p", 0, 3), ("xg", 3), ("t1", 0, 0), ("xf", 1), ("xf", 2), ("xf", 3),
+    ("t0", 2, 0), ("p", 1, 0), ("t1", 0, 1), ("p", 1, 1), ("t0", 3, 0), ("p", 1, 2), ("p", 1, 3),
+    ("xr", 0, 0), ("xr", 1, 0), ("t1", 4, "b"), ("t0", 1, 1), ("t0", 2, 1), ("xr", 0, 1), ("xr", 1, 1),
+    ("t2", 0, 0), ("t1", 1, 0), ("xf", 4), ("t0", 3, 1), ("t2", 0, 1), ("t1", 2, 0), ("xr", 0, 2),
+    ("xr", 1, 2), ("xf", 5), ("t2", 4, "b"), ("t1", 3, 0), ("b", 0), ("xr", 0, 3), ("xr", 1, 3), ("t2", 1, 0),
+    ("t1", 1, 1), ("xf", 6), ("t2", 2, 0), ("t1", 2, 1), ("xl", 0), ("t2", 3, 0), ("b", 1), ("t1", 3, 1),
+    ("xl", 1), ("t2", 1, 1), ("t3", 0), ("xr", 0, 4), ("xr", 1, 4), ("xf", 7), ("t3", 4), ("t2", 2, 1),
+    ("b", 2), ("xl", 2), ("t2", 3, 1), ("yl", 0), ("xr", 0, 5), ("xr", 1, 5), ("t4", 0), ("t3", 1), ("yl", 1),
+    ("t4", 4), ("t3", 2), ("rg", 0), ("t3", 3), ("b", 3), ("xl", 3), ("xr", 0, 6), ("xr", 1, 6), ("t4", 1),
+    ("yl", 2), ("zl", 0), ("b", 4), ("xl", 4), ("zl", 1), ("t4", 2), ("xr", 0, 7), ("xr", 1, 7), ("rg", 1),
+    ("t4", 3), ("rg", 2), ("xl", 5), ("rg", 3), ("g", 0), ("xl", 6), ("ns", 0), ("ns", 1), ("g", 1),
+    ("yl", 3), ("xl", 7), ("yl", 4), ("fr", 0), ("yl", 5), ("wr", 0), ("fr", 1), ("g", 2), ("wr", 1),
+    ("yl", 6), ("fr", 2), ("fr", 3), ("yl", 7), ("zl", 2), ("zl", 3), ("g", 3), ("zl", 4), ("zl", 5),
+    ("zl", 6), ("ns", 2), ("ns", 3), ("zl", 7), ("g", 4), ("wr", 2), ("g", 5), ("wr", 3), ("wr", 4),
+    ("wr", 5), ("wr", 6), ("wr", 7),
 )
 MESH = pl.DeviceIdType.MESH
 F32 = jnp.float32
@@ -308,6 +308,22 @@
         send(("xb", 0, k), part.at[k, xr, second_half], xin_b.at[0, k], d_x[1])
         send(("xb", 1, k), part.at[k, xl, first_half], xin_b.at[1, k], d_x[-1])
 
+    def x_early(g):
+        x2, xr, xl = mod(x + 2, 4), mod(x + 1, 4), mod(x - 1, 4)
+        for kind, way, q, half, into in (
+            ("xa", 0, x2, first_half, xin_a), ("xa", 1, x2, second_half, xin_a),
+            ("xb", 0, xr, second_half, xin_b), ("xb", 1, xl, first_half, xin_b),
+        ):
+            send((kind, way, 0, g), part.at[0, q, half, g], into.at[way, 0, pl.ds(0, 2), g],
+                 d_x[(1, -1)[way]])
+
+    def got_x(kind, way, k):
+        if k == 0:
+            for g in range(4):
+                got((kind, way, 0, g))
+        else:
+            got((kind, way, k))
+
     def add_into(k, q, half, *others):
         @pl.loop(0, 2, unroll=2)
         def _(i):
@@ -318,14 +334,14 @@
 
     def x_relay(way, k):
         q = mod(x + (1, -1)[way], 4)
-        got(("xa", way, k))
+        got_x("xa", way, k)
         add_into(k, q, way, xin_a.at[way, k])
         half = (first_half, second_half)[way]
         send(("xc", way, k), part.at[k, q, half], xin_c.at[way, k], d_x[(1, -1)[way]])
 
     def x_last(k):
         for way in range(2):
-            got(("xb", 1 - way, k))
+            got_x("xb", 1 - way, k)
             got(("xc", way, k))
             add_into(k, x, way, xin_c.at[way, k], xin_b.at[1 - way, k])
         for i, d in enumerate(deltas):
@@ -439,7 +455,11 @@
             piece(("ym", k), y_middle, k)
             piece(("xd", k), x_direct_last, k)
         else:
-            piece(("xf", k), x_first, k)
+            if k == 0:
+                for g in range(4):
+                    piece(("xg", g), x_early, g)
+            else:
+                piece(("xf", k), x_first, k)
             piece(("xr", 0, k), x_relay, 0, k)
             piece(("xr", 1, k), x_relay, 1, k)
             piece(("xl", k), x_last, k)
@@ -542,7 +562,7 @@
         copy.wait()
 
 
-MESSAGES = 298
+MESSAGES = 310
 
 
 def on_device(

time: 85.3 us -> 84.6 us (level)
  no operation moved by 1% of the time
where the time goes in v4:
time: 84.6 us; the launch traced here: 84.5 us
  Pallas kernels  77.5 us (92%)
  local copies, waits for them, and re-layouts  6.32 us (7%)
    pallas_call x1, Pallas kernels, on_device(): pl.pallas_call(kernel, out_shape=(jax.ShapeDtypeStruct((256, 8192), BF16)...  77.5 us
    unnamed x7, local copies, waits for them, and re-layouts  6.32 us

profile of v4, /device:TPU:1, one launch (start us, length us, event | category | flops | bytes accessed | tf_op | source)
XLA Modules:
  0.0 84.5 jit_solution(17519678767235724171)
XLA Ops:
  0.6 77.5 %shard_map.103 = (bf16[256,8192]{1,0:T(8,128)(2,1)}, f32[512,512]{1,0:T(8,128)}, f32[64,128]{1,0:T(8,128)}) custom-call(bf16[256,8192]{1,0:T(8,128)(2,1)} %tok_hbm.1, f32[64,128]{1,0:T(8,128)} %bitcast.6, bf16[2,256,512]{2,1,0:T(8,128)(2,1)} %bitcast.5, bf16[256,512]{1,0:T(8,128)(2,1)} %vg_ref.1, f32[2,128]{1,0:T(2,128)} %bitcast.8, f32[2,128]{1,0:T(2,128)} %bitcast.9, ...), custom_call_target="tpu_custom_call" | custom-call | tf_op jit(solution)/shard_map/pallas_call | solution.py:574
  78.2 0.0 copy-start
  78.2 0.0 copy-start.1
  78.2 4.7 %copy.14 = bf16[256,8192]{1,0:T(8,128)(2,1)} copy(bf16[256,8192]{1,0:T(8,128)(2,1)} %get-tuple-element.12) | data formatting | bytes 8388608
  82.9 0.0 copy-done
  82.9 1.0 %copy.15 = f32[512,512]{1,0:T(8,128)} copy(f32[512,512]{1,0:T(8,128)S(1)} %copy-done) | data formatting | bytes 2097152
  83.9 0.0 copy-done.1
  83.9 0.6 copy.16
Async XLA Ops:
  78.2 4.7 %copy-start = (f32[512,512]{1,0:T(8,128)S(1)}, f32[512,512]{1,0:T(8,128)}, u32[]{:S(2)}) copy-start(f32[512,512]{1,0:T(8,128)} %get-tuple-element.13) | copy-start | bytes 3145732
  78.2 5.7 %copy-start.1 = (f32[64,128]{1,0:T(8,128)S(1)}, f32[64,128]{1,0:T(8,128)}, u32[]{:S(2)}) copy-start(f32[64,128]{1,0:T(8,128)} %get-tuple-element.8) | copy-start | bytes 98308

commit v5 on v4

--- a/solution.py
+++ b/solution.py
@@ -11,26 +11,26 @@
 EPS = 1e-06
 K = 8
 R = 128 // K
-YF = ()
-FAST = 4
-CUT = 160
+YF = (7,)
+FAST = 2
+CUT = 192
 ORDER = (
     ("t0", 0, 0), ("t0", 0, 1), ("t0", 4, "b"), ("p", 0, 0), ("xg", 0), ("p", 0, 1), ("xg", 1), ("p", 0, 2),
-    ("xg", 2), ("t0", 1, 0), ("p", 0, 3), ("xg", 3), ("t1", 0, 0), ("xf", 1), ("xf", 2), ("xf", 3),
-    ("t0", 2, 0), ("p", 1, 0), ("t1", 0, 1), ("p", 1, 1), ("t0", 3, 0), ("p", 1, 2), ("p", 1, 3),
-    ("xr", 0, 0), ("xr", 1, 0), ("t1", 4, "b"), ("t0", 1, 1), ("t0", 2, 1), ("xr", 0, 1), ("xr", 1, 1),
-    ("t2", 0, 0), ("t1", 1, 0), ("xf", 4), ("t0", 3, 1), ("t2", 0, 1), ("t1", 2, 0), ("xr", 0, 2),
-    ("xr", 1, 2), ("xf", 5), ("t2", 4, "b"), ("t1", 3, 0), ("b", 0), ("xr", 0, 3), ("xr", 1, 3), ("t2", 1, 0),
-    ("t1", 1, 1), ("xf", 6), ("t2", 2, 0), ("t1", 2, 1), ("xl", 0), ("t2", 3, 0), ("b", 1), ("t1", 3, 1),
-    ("xl", 1), ("t2", 1, 1), ("t3", 0), ("xr", 0, 4), ("xr", 1, 4), ("xf", 7), ("t3", 4), ("t2", 2, 1),
-    ("b", 2), ("xl", 2), ("t2", 3, 1), ("yl", 0), ("xr", 0, 5), ("xr", 1, 5), ("t4", 0), ("t3", 1), ("yl", 1),
-    ("t4", 4), ("t3", 2), ("rg", 0), ("t3", 3), ("b", 3), ("xl", 3), ("xr", 0, 6), ("xr", 1, 6), ("t4", 1),
-    ("yl", 2), ("zl", 0), ("b", 4), ("xl", 4), ("zl", 1), ("t4", 2), ("xr", 0, 7), ("xr", 1, 7), ("rg", 1),
-    ("t4", 3), ("rg", 2), ("xl", 5), ("rg", 3), ("g", 0), ("xl", 6), ("ns", 0), ("ns", 1), ("g", 1),
-    ("yl", 3), ("xl", 7), ("yl", 4), ("fr", 0), ("yl", 5), ("wr", 0), ("fr", 1), ("g", 2), ("wr", 1),
-    ("yl", 6), ("fr", 2), ("fr", 3), ("yl", 7), ("zl", 2), ("zl", 3), ("g", 3), ("zl", 4), ("zl", 5),
-    ("zl", 6), ("ns", 2), ("ns", 3), ("zl", 7), ("g", 4), ("wr", 2), ("g", 5), ("wr", 3), ("wr", 4),
-    ("wr", 5), ("wr", 6), ("wr", 7),
+    ("xg", 2), ("p", 0, 3), ("xg", 3), ("t1", 0, 0), ("t0", 1, 0), ("t0", 2, 0), ("xf", 1), ("xf", 2),
+    ("xf", 3), ("p", 1, 0), ("p", 1, 1), ("p", 1, 2), ("t1", 0, 1), ("p", 1, 3), ("xr", 0, 0), ("xr", 1, 0),
+    ("t0", 3, 0), ("t1", 4, "b"), ("yf", 7), ("t0", 1, 1), ("t0", 2, 1), ("xr", 0, 1), ("xr", 1, 1),
+    ("t2", 0, 0), ("xf", 4), ("t1", 1, 0), ("t0", 3, 1), ("t2", 0, 1), ("xr", 0, 2), ("xr", 1, 2),
+    ("t1", 2, 0), ("xf", 5), ("t2", 4, "b"), ("b", 0), ("t1", 3, 0), ("xr", 0, 3), ("xr", 1, 3), ("t2", 1, 0),
+    ("xf", 6), ("t1", 1, 1), ("b", 1), ("t2", 2, 0), ("xl", 0), ("t1", 2, 1), ("xl", 1), ("t2", 3, 0),
+    ("xr", 0, 4), ("xr", 1, 4), ("t1", 3, 1), ("t2", 1, 1), ("ym", 7), ("t3", 0), ("xl", 2), ("t3", 4),
+    ("t2", 2, 1), ("xr", 0, 5), ("xr", 1, 5), ("b", 2), ("t2", 3, 1), ("t3", 1), ("yl", 0), ("xl", 3),
+    ("t4", 0), ("yl", 1), ("t4", 4), ("t3", 2), ("xr", 0, 6), ("xr", 1, 6), ("rg", 0), ("t3", 3), ("b", 3),
+    ("t4", 1), ("xl", 4), ("yl", 2), ("yl", 3), ("xd", 7), ("b", 4), ("xl", 5), ("t4", 2), ("rg", 1),
+    ("rg", 2), ("t4", 3), ("xl", 6), ("yl", 4), ("rg", 3), ("g", 0), ("yl", 5), ("g", 1), ("zl", 0),
+    ("zl", 1), ("zl", 2), ("yl", 6), ("zl", 3), ("zl", 4), ("g", 2), ("ns", 0), ("zl", 7), ("ns", 1),
+    ("zl", 5), ("ns", 2), ("fr", 0), ("fr", 1), ("ns", 3), ("fr", 2), ("ns", 4), ("fr", 3), ("g", 3),
+    ("zl", 6), ("ns", 5), ("wr", 0), ("wr", 1), ("wr", 2), ("wr", 3), ("wr", 4), ("g", 4), ("wr", 5),
+    ("wr", 6), ("wr", 7), ("g", 5),
 )
 MESH = pl.DeviceIdType.MESH
 F32 = jnp.float32
@@ -562,7 +562,7 @@
         copy.wait()
 
 
-MESSAGES = 310
+MESSAGES = 305
 
 
 def on_device(

time: 84.6 us -> 84.8 us (level)
  no operation moved by 1% of the time
where the time goes in v5:
time: 84.8 us; the launch traced here: 84.7 us
  Pallas kernels  77.7 us (92%)
  local copies, waits for them, and re-layouts  6.32 us (7%)
    pallas_call x1, Pallas kernels, on_device(): pl.pallas_call(kernel, out_shape=(jax.ShapeDtypeStruct((256, 8192), BF16)...  77.7 us
    unnamed x7, local copies, waits for them, and re-layouts  6.32 us

profile of v5, /device:TPU:1, one launch (start us, length us, event | category | flops | bytes accessed | tf_op | source)
XLA Modules:
  0.0 84.7 jit_solution(3032478278017759545)
XLA Ops:
  0.6 77.7 %shard_map.103 = (bf16[256,8192]{1,0:T(8,128)(2,1)}, f32[512,512]{1,0:T(8,128)}, f32[64,128]{1,0:T(8,128)}) custom-call(bf16[256,8192]{1,0:T(8,128)(2,1)} %tok_hbm.1, f32[64,128]{1,0:T(8,128)} %bitcast.6, bf16[2,256,512]{2,1,0:T(8,128)(2,1)} %bitcast.5, bf16[256,512]{1,0:T(8,128)(2,1)} %vg_ref.1, f32[2,128]{1,0:T(2,128)} %bitcast.8, f32[2,128]{1,0:T(2,128)} %bitcast.9, ...), custom_call_target="tpu_custom_call" | custom-call | tf_op jit(solution)/shard_map/pallas_call | solution.py:574
  78.4 0.0 copy-start
  78.4 0.0 copy-start.1
  78.4 4.7 %copy.14 = bf16[256,8192]{1,0:T(8,128)(2,1)} copy(bf16[256,8192]{1,0:T(8,128)(2,1)} %get-tuple-element.12) | data formatting | bytes 8388608
  83.1 0.0 copy-done
  83.1 1.0 %copy.15 = f32[512,512]{1,0:T(8,128)} copy(f32[512,512]{1,0:T(8,128)S(1)} %copy-done) | data formatting | bytes 2097152
  84.1 0.0 copy-done.1
  84.1 0.6 copy.16
Async XLA Ops:
  78.4 4.7 %copy-start = (f32[512,512]{1,0:T(8,128)S(1)}, f32[512,512]{1,0:T(8,128)}, u32[]{:S(2)}) copy-start(f32[512,512]{1,0:T(8,128)} %get-tuple-element.13) | copy-start | bytes 3145732
  78.4 5.7 %copy-start.1 = (f32[64,128]{1,0:T(8,128)S(1)}, f32[64,128]{1,0:T(8,128)}, u32[]{:S(2)}) copy-start(f32[64,128]{1,0:T(8,128)} %get-tuple-element.8) | copy-start | bytes 98308
